TPU v7x, 32 devices: a whole 2x2x4 slice. The times are simulated.
32 devices in a mesh: seq: 4 (over y, x), fsdp: 4 (over z), grp: 2 (over core).
Axes of the slice: x: 2, y: 2, z: 4, core: 2. Of those that a mesh axis runs over, the one named last changes fastest.
Arguments:
- queries: bfloat16 [1, 2048, 2048], P(None, ('seq', 'fsdp'), 'grp'), may hold values from -208 to 208
- encodings: bfloat16 [1, 32, 2, 128, 896], P(None, ('seq', 'fsdp'), None, 'grp'), may hold values from -6 to 6
- neighbour_lengths: int32 [1, 32, 2], P(None, ('seq', 'fsdp')), may hold values from 32 to 128
- key_weight: bfloat16 [896, 2048], P(None, 'grp'), may hold values from -0.1875 to 0.1875
- value_weight: bfloat16 [896, 2048], P(None, 'grp'), may hold values from -0.1875 to 0.1875
Outputs:
- attended: bfloat16 [1, 2048, 2048], P(None, ('seq', 'fsdp'), 'grp')
All inputs are finite; a program needn't handle non-finite values.
Results may differ from a plain program's by a relative error of at most 0.011.
Values may be sent and summed in bfloat16 or wider, within the bound.
No kernel may reach another device: no remote copies, remote signals or barrier semaphores. Data moves between devices by JAX's collectives and lax.ppermute only.
A program may use at most 64 MiB of HBM per device.

v0:
```python
import jax
import jax.numpy as jnp
from jax import lax
from jax.sharding import PartitionSpec as P

HEAD_DIM = 128


mask_fill = -1e30


def shifted(array, axis, by):
    size = lax.axis_size(axis)
    pairs = [(i, i + by) for i in range(size) if 0 <= i + by < size]
    return lax.ppermute(array, axis, pairs)


def attend_blocks(query_blocks, key_value, lengths):
    seq_count, block_count, row_count, col_count = query_blocks.shape
    head_count = col_count // HEAD_DIM
    key_count = key_value.shape[3] * key_value.shape[4]
    softmax_scale = HEAD_DIM ** (-0.5)
    query_heads = query_blocks.reshape(seq_count, block_count, row_count, head_count, HEAD_DIM)
    key_rows = key_value[0].reshape(seq_count, block_count, key_count, head_count, HEAD_DIM)
    value_rows = key_value[1].reshape(seq_count, block_count, key_count, head_count, HEAD_DIM)
    scores = (
        jnp.einsum("bnqhd,bnkhd->bnhqk", query_heads, key_rows, preferred_element_type=jnp.float32)
        * softmax_scale
    )
    position = lax.broadcasted_iota(jnp.float32, key_value.shape[1:5], 3)
    key_live = (position < lengths[..., None]).reshape(seq_count, block_count, 1, 1, key_count)
    scores = jnp.where(key_live, scores, mask_fill)
    row_max = jnp.max(scores, axis=-1, keepdims=True)
    weights = jnp.exp(scores - row_max)
    attention = (weights / jnp.sum(weights, axis=-1, keepdims=True)).astype(jnp.bfloat16)
    attended = jnp.einsum(
        "bnhqk,bnkhd->bnqhd", attention, value_rows, preferred_element_type=jnp.float32
    )
    return attended.astype(jnp.bfloat16).reshape(seq_count, block_count * row_count, col_count)


def attend_padded(queries, all_pairs, all_lengths, group_count, group_len):
    seq_count, tok_count, col_count = queries.shape
    lead_zeros = jnp.zeros((seq_count, 1, col_count), jnp.bfloat16)
    trail_zeros = jnp.zeros((seq_count, group_len - 1, col_count), jnp.bfloat16)
    padded = jnp.concatenate([lead_zeros, queries, trail_zeros], axis=1)
    blocks = padded.reshape(seq_count, group_count + 1, group_len, col_count)
    attended = attend_blocks(blocks, all_pairs, all_lengths)
    return attended[:, 1 : 1 + tok_count]


def shards(queries, encodings, neighbour_lengths, key_weight, value_weight):
    seq_count, tok_count, col_count = queries.shape
    group_count = encodings.shape[1]
    group_len = tok_count // group_count
    enc_width = encodings.shape[4]
    lengths = neighbour_lengths.astype(jnp.float32)
    shard_rows = lax.all_gather(encodings, "grp", axis=3, tiled=True)
    flat_rows = shard_rows.reshape(-1, enc_width)
    key_part = jnp.dot(flat_rows, key_weight, preferred_element_type=jnp.float32).astype(
        jnp.bfloat16
    )
    value_part = jnp.dot(flat_rows, value_weight, preferred_element_type=jnp.float32).astype(
        jnp.bfloat16
    )
    key_value = jnp.stack([key_part, value_part]).reshape(
        (2,) + shard_rows.shape[:4] + (col_count,)
    )
    last_pair = key_value[:, :, group_count - 1]
    last_lengths = neighbour_lengths[:, group_count - 1].astype(jnp.bfloat16)
    prev_pair, prev_lengths = shifted((last_pair, last_lengths), ("seq", "fsdp"), 1)
    all_pairs = jnp.concatenate([prev_pair[:, :, None], key_value], axis=2)
    all_lengths = jnp.concatenate([prev_lengths.astype(jnp.float32)[:, None], lengths], axis=1)
    return attend_padded(queries, all_pairs, all_lengths, group_count, group_len)


def solution(mesh):
    placed = (
        P(None, ("seq", "fsdp"), "grp"),
        P(None, ("seq", "fsdp"), None, "grp", None),
        P(None, ("seq", "fsdp"), None),
        P(None, "grp"),
        P(None, "grp"),
    )
    return jax.shard_map(
        shards,
        mesh=mesh,
        in_specs=placed,
        out_specs=P(None, ("seq", "fsdp"), "grp"),
        check_vma=False,
    )
```

profile of v0, /device:TPU:5, one launch (start us, length us, event | category | flops | bytes accessed | tf_op | source)
XLA Modules:
  0.0 47.0 jit_solution(3821318916086933471)
XLA Ops:
  0.0 0.0 copy-start
  0.0 3.1 %all_gather.3 = bf16[1,2,2,128,896]{4,3,2,1,0:T(8,128)(2,1)S(1)} all-gather(bf16[1,2,2,64,896]{4,3,2,1,0:T(8,128)(2,1)} %param.6), channel_id=1, replica_groups=mesh['seq'=4,'fsdp'=4,'grp'=2] {'grp'}, dimensions={3}, use_global_device_ids=true | all-gather | bytes 1376256 | tf_op jit(solution)/shard_map/all_gather | solution.py:58
  3.1 0.0 copy-done
  3.1 0.0 copy-start.3
  3.1 1.3 %convolution_convert_fusion.1 = bf16[512,1024]{1,0:T(8,128)(2,1)S(1)} fusion(bf16[512,896]{1,0:T(8,128)(2,1)S(1)} %bitcast.59, bf16[896,1024]{1,0:T(8,128)(2,1)S(1)} %copy-done), kind=kOutput, calls=%fused_computation.11 | convolution fusion | flops 940048384 | bytes 3801088 | tf_op jit(solution)/shard_map/dot_general | solution.py:60
  4.4 0.2 copy-done.3
  4.6 1.2 %convolution_convert_fusion = bf16[512,1024]{1,0:T(8,128)(2,1)S(1)} fusion(bf16[512,896]{1,0:T(8,128)(2,1)S(1)} %bitcast.60, bf16[896,1024]{1,0:T(8,128)(2,1)S(1)} %copy-done.3), kind=kOutput, calls=%fused_computation.10 | convolution fusion | flops 940048384 | bytes 3801088 | tf_op jit(solution)/shard_map/dot_general | solution.py:63
  5.9 0.0 copy-start.2
  5.9 0.0 copy-start.1
  5.9 0.1 fusion.15
  6.0 3.2 %collective-permute-start = (bf16[2,1,2,128,1024]{4,3,2,0,1:T(8,128)(2,1)S(1)}, bf16[2,1,2,128,1024]{4,3,2,0,1:T(8,128)(2,1)S(1)}, u32[]{:S(2)}, u32[]{:S(2)}) collective-permute-start(bf16[2,1,2,128,1024]{4,3,2,0,1:T(8,128)(2,1)S(1)} %fusion.15), channel_id=1, source_target_pairs={{0,2},{2,4},{4,6},{6,8},{8,10},{10,12},{12,14},{14,16},{16,18},{18... | collective-permute-start | bytes 3145736 | tf_op jit(solution)/shard_map/ppermute | solution.py:15
  9.2 0.0 copy-done.2
  9.2 3.2 %collective-permute-start.1 = (bf16[1,2]{1,0:T(2,128)(2,1)S(1)}, bf16[1,2]{1,0:T(2,128)(2,1)S(1)}, u32[]{:S(2)}, u32[]{:S(2)}) collective-permute-start(bf16[1,2]{1,0:T(2,128)(2,1)S(1)} %slice_bitcast_fusion), channel_id=1, source_target_pairs={{0,2},{2,4},{4,6},{6,8},{8,10},{10,12},{12,14},{14,16},{16,18},{18... | collective-permute-start | bytes 20 | tf_op jit(solution)/shard_map/ppermute | solution.py:15
  12.5 0.1 pad.7.clone
  12.5 0.0 copy-done.1
  12.5 0.2 maximum_bitcast_fusion
  12.8 0.1 copy.18
  12.8 23.0 %collective-permute-done.1 = bf16[1,2]{1,0:T(2,128)(2,1)S(1)} collective-permute-done((bf16[1,2]{1,0:T(2,128)(2,1)S(1)}, bf16[1,2]{1,0:T(2,128)(2,1)S(1)}, u32[]{:S(2)}, u32[]{:S(2)}) %collective-permute-start.1) | collective-permute-done | bytes 36 | tf_op jit(solution)/shard_map/ppermute | solution.py:15
  35.9 0.1 broadcast_bitcast_fusion
  36.0 0.0 collective-permute-done
  36.0 0.3 maximum_maximum_fusion
  36.3 0.3 fusion.19
  36.6 0.4 copy.19
  37.1 0.7 %multiply_select_fusion = f32[3,8,64,256]{3,2,1,0:T(8,128)S(1)} fusion(bf16[3,256,8,128]{3,2,1,0:T(8,128)(2,1)S(1)} %bitcast.51, pred[3,256]{1,0:T(4,128)(4,1)S(1)} %bitcast_compare_fusion, bf16[3,64,8,128]{3,2,1,0:T(8,128)(2,1)S(1)} %bitcast.57), kind=kOutput, calls=%fused_computation.8 | convolution fusion | flops 101449728 | bytes 3539712 | tf_op jit(solution)/shard_map/bnqhd,bnkhd->bnhqk/dot_general | solution.py:27
  37.7 0.5 %fusion.21 = f32[3,8,64]{2,1,0:T(8,128)S(1)} fusion(f32[3,8,64,256]{3,2,1,0:T(8,128)S(1)} %multiply_select_fusion), kind=kOutput, calls=%fused_computation.28 | output fusion | flops 786687 | bytes 1579008 | tf_op jit(solution)/shard_map/sub | solution.py:34
  38.2 1.6 %copy.20 = bf16[96,8,8,128]{3,2,1,0:T(8,128)(2,1)} copy(bf16[96,8,8,128]{3,1,2,0:T(8,128)(2,1)S(1)} %bitcast.49) | data formatting | bytes 3145728
  39.8 4.9 %fusion.12 = bf16[1,3,64,8,128]{4,2,3,1,0:T(8,128)(2,1)} fusion(bf16[3,256,8,128]{3,2,1,0:T(8,128)(2,1)} %bitcast.56, f32[3,8,64]{2,1,0:T(8,128)S(1)} %fusion.21, f32[3,8,64,256]{3,2,1,0:T(8,128)S(1)} %multiply_select_fusion), kind=kOutput, calls=%fused_computation.13 | convolution fusion | flops 102041344 | bytes 3545088 | tf_op jit(solution)/shard_map/bnhqk,bnkhd->bnqhd/dot_general | solution.py:36
  44.8 1.3 %copy.15 = bf16[1,3,64,8,128]{4,3,2,1,0:T(8,128)(2,1)S(1)} copy(bf16[1,3,64,8,128]{4,2,3,1,0:T(8,128)(2,1)} %fusion.12) | data formatting | bytes 786432 | tf_op jit(solution)/shard_map/convert_element_type | solution.py:39
  46.0 0.2 reshape.85
  46.2 0.8 %slice.23 = bf16[1,128,1024]{2,1,0:T(8,128)(2,1)} slice(bf16[1,192,1024]{2,1,0:T(8,128)(2,1)S(1)} %reshape.85), slice={[0:1], [1:129], [0:1024]} | slice | bytes 524288 | tf_op jit(solution)/shard_map/slice | solution.py:49
  (8 shorter events, 0.1 us)
Async XLA Ops:
  0.0 3.1 %copy-start = (bf16[896,1024]{1,0:T(8,128)(2,1)S(1)}, bf16[896,1024]{1,0:T(8,128)(2,1)}, u32[]{:S(2)}) copy-start(bf16[896,1024]{1,0:T(8,128)(2,1)} %param.8) | copy-start | bytes 5505028
  3.1 1.5 %copy-start.3 = (bf16[896,1024]{1,0:T(8,128)(2,1)S(1)}, bf16[896,1024]{1,0:T(8,128)(2,1)}, u32[]{:S(2)}) copy-start(bf16[896,1024]{1,0:T(8,128)(2,1)} %param.9) | copy-start | bytes 5505028
  5.9 3.3 %copy-start.2 = (s32[1,2,2]{2,1,0:T(2,128)S(1)}, s32[1,2,2]{2,1,0:T(2,128)}, u32[]{:S(2)}) copy-start(s32[1,2,2]{2,1,0:T(2,128)} %param.7) | copy-start | bytes 52
  5.9 6.7 %copy-start.1 = (bf16[1,128,1024]{2,1,0:T(8,128)(2,1)S(1)}, bf16[1,128,1024]{2,1,0:T(8,128)(2,1)}, u32[]{:S(2)}) copy-start(bf16[1,128,1024]{2,1,0:T(8,128)(2,1)} %param.5) | copy-start | bytes 786436
  6.0 30.0 %collective-permute-start = (bf16[2,1,2,128,1024]{4,3,2,0,1:T(8,128)(2,1)S(1)}, bf16[2,1,2,128,1024]{4,3,2,0,1:T(8,128)(2,1)S(1)}, u32[]{:S(2)}, u32[]{:S(2)}) collective-permute-start(bf16[2,1,2,128,1024]{4,3,2,0,1:T(8,128)(2,1)S(1)} %fusion.15), channel_id=1, source_target_pairs={{0,2},{2,4},{4,6},{6,8},{8,10},{10,12},{12,14},{14,16},{16,18},{18... | collective-permute-start | bytes 3145736 | tf_op jit(solution)/shard_map/ppermute | solution.py:15
  9.2 26.6 %collective-permute-start.1 = (bf16[1,2]{1,0:T(2,128)(2,1)S(1)}, bf16[1,2]{1,0:T(2,128)(2,1)S(1)}, u32[]{:S(2)}, u32[]{:S(2)}) collective-permute-start(bf16[1,2]{1,0:T(2,128)(2,1)S(1)} %slice_bitcast_fusion), channel_id=1, source_target_pairs={{0,2},{2,4},{4,6},{6,8},{8,10},{10,12},{12,14},{14,16},{16,18},{18... | collective-permute-start | bytes 20 | tf_op jit(solution)/shard_map/ppermute | solution.py:15
where the time goes:
time: 47.8 us; the launch traced here: 47 us
  waiting for transfers between devices  23 us (48%)
  matrix products  8.11 us (17%)
  starting transfers between devices  6.41 us (13%)
  local copies, waits for them, and re-layouts  5.01 us (10%)
  blocking collectives  3.09 us (6%)
  other arithmetic  1.15 us (2%)
    ppermute x2, waiting for transfers between devices, shifted(): return lax.ppermute(array, axis, pairs)  23 us
    ppermute x2, starting transfers between devices, shifted(): return lax.ppermute(array, axis, pairs)  6.41 us
    dot_general x1, matrix products, attend_blocks(): jnp.einsum('bnhqk,bnkhd->bnqhd', attention, value_rows, preferred_element...  4.9 us
    all_gather x1, blocking collectives, shards(): shard_rows = lax.all_gather(encodings, 'grp', axis=3, tiled=True)  3.09 us
    unnamed x12, local copies, waits for them, and re-layouts  2.41 us
    dot_general x1, matrix products, shards(): jnp.dot(flat_rows, key_weight, preferred_element_type=jnp.float32)  1.29 us
    convert_element_type x1, local copies, waits for them, and re-layouts, attend_blocks(): attended.astype(jnp.bfloat16)  1.25 us
    dot_general x1, matrix products, shards(): jnp.dot(flat_rows, value_weight, preferred_element_type=jnp.float32)  1.25 us
  transfers between devices with their start and end apart: 2, of which 1 were waited for; matrix products, arithmetic and copies ran while one was open for 1% of the time, Pallas kernels for 0%

commit v1 on v0

v1 whole, which is shorter than its diff:
```python
import math

import jax
import jax.numpy as jnp
from jax import lax
from jax.experimental import pallas as pl
from jax.experimental.pallas import tpu as pltpu
from jax.sharding import PartitionSpec as P

HEAD_DIM = 128
MASK_FILL = -1e30
SCORE_SCALE = HEAD_DIM ** (-0.5) * math.log2(math.e)
DEAD = 8.0
AXES = ("seq", "fsdp")


def dot(a, b):
    return jnp.dot(a, b, preferred_element_type=jnp.float32)


def dot_nt(a, b):
    return lax.dot_general(a, b, (((1,), (1,)), ((), ())), preferred_element_type=jnp.float32)


def softmax_weights(scores, dead):
    scores = jnp.where(dead, MASK_FILL, scores * SCORE_SCALE)
    return jnp.exp2(scores - jnp.max(scores, axis=-1, keepdims=True)).astype(jnp.bfloat16)


def mix(weights, rows):
    ones = jnp.ones((rows.shape[0], 128), jnp.bfloat16)
    mixed = dot(weights, jnp.concatenate([rows, ones], axis=1))
    return mixed[:, :-128] * (1.0 / mixed[:, -1:])


def payload_kernel(length_hbm, enc_hbm, out_ref, dead_ref, length_ref, sems):
    group_count, neighbours, nb_half, _ = enc_hbm.shape[1:]
    copies = [
        pltpu.make_async_copy(length_hbm, length_ref, sems.at[0]),
        pltpu.make_async_copy(enc_hbm.at[0, group_count - 1], out_ref, sems.at[1]),
    ]
    for copy in copies:
        copy.start()
    core = lax.axis_index("grp")
    key = lax.broadcasted_iota(jnp.int32, (1, 2 * neighbours * nb_half), 1)
    row = lax.broadcasted_iota(jnp.int32, (nb_half, 128), 0) + core * nb_half
    lane = lax.broadcasted_iota(jnp.int32, (nb_half, 128), 1)
    copies[0].wait()

    def length(g, n):
        return length_ref[0, g : g + 1, n : n + 1]

    for g in range(group_count):
        ends = [jnp.broadcast_to(length(g, n), key.shape) for n in range(neighbours)]
        dead = jnp.zeros(key.shape, jnp.int32)
        for block in range(2 * neighbours):
            place = key - block * nb_half
            here = (place >= 0) & (place < nb_half)
            dead = jnp.where(here & (place + block // neighbours * nb_half >= ends[block % neighbours]), 1, dead)
        dead_ref[pl.ds(g, 1), :] = dead
    marks = [
        (lane == 0) & (row >= jnp.broadcast_to(length(group_count - 1, n), row.shape)) for n in range(neighbours)
    ]
    copies[1].wait()
    for n in range(neighbours):
        part = out_ref[n, :, :128].astype(jnp.float32)
        out_ref[n, :, :128] = jnp.where(marks[n], DEAD, part).astype(jnp.bfloat16)


def local_kernel(dead_ref, query_ref, enc_ref, kw_ref, vw_ref, out_ref, map_ref):
    tok_count, col_count = query_ref.shape[1:]
    head_count = col_count // HEAD_DIM
    neighbours, nb_half, enc_width = enc_ref.shape[3:]
    half = neighbours * nb_half
    glen = tok_count // 2

    def group(g):
        rows = [enc_ref[core, 0, g].reshape(half, enc_width) for core in range(2)]
        return jnp.concatenate(rows, axis=0), dead_ref[g : g + 1, :] > 0

    query = pltpu.roll(query_ref[0].astype(jnp.float32), 1, 0).astype(jnp.bfloat16)

    head_row = lax.broadcasted_iota(jnp.int32, (16, 1), 0)
    row = lax.broadcasted_iota(jnp.int32, (glen, enc_width), 0)
    lane = lax.broadcasted_iota(jnp.int32, (1, enc_width), 1)
    one_hot = jnp.where(lane == 0, 1.0, 0.0)
    last = jnp.zeros((16, enc_width), jnp.float32)
    for h in range(head_count):
        cols = slice(h * HEAD_DIM, (h + 1) * HEAD_DIM)
        mapped = dot_nt(query[:glen, cols], kw_ref[:, cols])
        last = jnp.where(head_row == h, mapped[0:1], last)
        map_ref[pl.ds(h * glen, glen), :] = jnp.where(row == 0, one_hot, mapped).astype(jnp.bfloat16)

    enc, dead = group(1)
    last = mix(softmax_weights(dot_nt(last.astype(jnp.bfloat16), enc), dead), enc).astype(jnp.bfloat16)

    enc, dead = group(0)
    value_lhs = jnp.concatenate([enc, last], axis=0)
    wide = 2 * HEAD_DIM
    for c in range(col_count // wide):
        cols = slice(c * wide, (c + 1) * wide)
        keys = dot(enc, kw_ref[:, cols]).astype(jnp.bfloat16)
        values = dot(value_lhs, vw_ref[:, cols])
        last_out = values[2 * half :]
        values = values[: 2 * half].astype(jnp.bfloat16)
        for i in range(2):
            h = 2 * c + i
            cols = slice(h * HEAD_DIM, (h + 1) * HEAD_DIM)
            own = slice(i * HEAD_DIM, (i + 1) * HEAD_DIM)
            weights = softmax_weights(dot_nt(query[glen:, cols], keys[:, own]), dead)
            out = mix(weights, values[:, own])
            first = jnp.broadcast_to(last_out[h : h + 1, own], (glen, HEAD_DIM))
            out = pltpu.roll(jnp.concatenate([first, out], axis=0), tok_count - 1, 0)
            out_ref[:, cols] = out.astype(jnp.bfloat16)


def own_value_kernel(own_ref, vw_ref, value_ref):
    value_ref[...] = dot(own_ref[...].reshape(-1, own_ref.shape[-1]), vw_ref[...]).astype(jnp.bfloat16)


def halo_kernel(own_ref, other_ref, own_value_ref, map_ref, vw_ref, mid_ref, out_hbm, score_ref, top_ref, sems):
    tok_count, col_count = mid_ref.shape
    glen = tok_count // 2
    enc_width = own_ref.shape[-1]
    row = lax.broadcasted_iota(jnp.int32, (glen, 1), 0)
    is_first = lax.axis_index(AXES) == 0
    rest = pltpu.make_async_copy(mid_ref.at[pl.ds(glen, glen)], out_hbm.at[0, pl.ds(glen, glen)], sems.at[0])
    rest.start()

    @pl.when(is_first)
    def _():
        edge = mid_ref[:glen, :].astype(jnp.float32)
        top_ref[...] = jnp.where(row < glen - 1, 0.0, edge).astype(jnp.bfloat16)

    @pl.when(jnp.logical_not(is_first))
    def _():
        own, other = (ref[...].reshape(-1, enc_width) for ref in (own_ref, other_ref))
        score_ref[...] = dot_nt(map_ref[...], jnp.concatenate([own, other], axis=0))
        dead = score_ref[0:1, :] > DEAD - 1.0
        for start in range(0, col_count, 2 * HEAD_DIM):
            wide = slice(start, start + 2 * HEAD_DIM)
            other_value = dot(other, vw_ref[:, wide]).astype(jnp.bfloat16)
            value = jnp.concatenate([own_value_ref[:, wide], other_value], axis=0)
            for i in range(2):
                h = start // HEAD_DIM + i
                cols = slice(h * HEAD_DIM, (h + 1) * HEAD_DIM)
                weights = softmax_weights(score_ref[pl.ds(h * glen, glen), :], dead)
                out = mix(weights, value[:, i * HEAD_DIM : (i + 1) * HEAD_DIM])
                out = pltpu.roll(out, glen - 1, 0)
                out = jnp.where(row < glen - 1, out, mid_ref[:glen, cols].astype(jnp.float32))
                top_ref[:, cols] = out.astype(jnp.bfloat16)

    top = pltpu.make_async_copy(top_ref, out_hbm.at[0, pl.ds(0, glen)], sems.at[1])
    top.start()
    rest.wait()
    top.wait()


def shards(queries, encodings, neighbour_lengths, key_weight, value_weight):
    tok_count, col_count = queries.shape[1:]
    group_count, neighbours, nb_half, enc_width = encodings.shape[1:]
    key_count = 2 * neighbours * nb_half
    glen = tok_count // group_count
    rows = col_count // HEAD_DIM * glen
    vmem = pl.BlockSpec(memory_space=pltpu.VMEM)
    hbm = pl.BlockSpec(memory_space=pltpu.HBM)
    params = pltpu.CompilerParams(vmem_limit_bytes=24 * 2**20)

    payload, dead = pl.pallas_call(
        payload_kernel,
        out_shape=[
            jax.ShapeDtypeStruct((neighbours, nb_half, enc_width), jnp.bfloat16),
            jax.ShapeDtypeStruct((group_count, key_count), jnp.int32),
        ],
        in_specs=[hbm, hbm],
        out_specs=[vmem, vmem],
        scratch_shapes=[pltpu.VMEM(neighbour_lengths.shape, jnp.int32), pltpu.SemaphoreType.DMA((2,))],
        compiler_params=pltpu.CompilerParams(vmem_limit_bytes=4 * 2**20),
        cost_estimate=pl.CostEstimate(flops=10**10, bytes_accessed=2**20, transcendentals=0),
        name="payload",
    )(*(pltpu.with_memory_space_constraint(x, pltpu.HBM) for x in (neighbour_lengths, encodings)))
    size = lax.axis_size(AXES)
    halo = lax.ppermute(payload, AXES, [(i, (i + 1) % size) for i in range(size)])
    enc = lax.all_gather(encodings, "grp", axis=0)
    mid, mapped = pl.pallas_call(
        local_kernel,
        out_shape=[
            jax.ShapeDtypeStruct((tok_count, col_count), jnp.bfloat16),
            jax.ShapeDtypeStruct((rows, enc_width), jnp.bfloat16),
        ],
        in_specs=[vmem] * 5,
        out_specs=[vmem] * 2,
        compiler_params=params,
        cost_estimate=pl.CostEstimate(flops=2 * 10**9, bytes_accessed=6 * 2**20, transcendentals=0),
        name="local_groups",
    )(dead, queries, enc, key_weight, value_weight)

    halo, mid, mapped = lax.optimization_barrier((halo, mid, mapped))
    halo_other = lax.ppermute(halo, "grp", [(0, 1), (1, 0)])
    own_value = pl.pallas_call(
        own_value_kernel,
        out_shape=jax.ShapeDtypeStruct((neighbours * nb_half, col_count), jnp.bfloat16),
        in_specs=[vmem] * 2,
        out_specs=vmem,
        compiler_params=params,
        cost_estimate=pl.CostEstimate(flops=3 * 10**8, bytes_accessed=2**20, transcendentals=0),
        name="own_values",
    )(halo, value_weight)
    return pl.pallas_call(
        halo_kernel,
        out_shape=jax.ShapeDtypeStruct(queries.shape, jnp.bfloat16),
        in_specs=[vmem] * 6,
        out_specs=hbm,
        scratch_shapes=[
            pltpu.VMEM((rows, key_count), jnp.float32),
            pltpu.VMEM((glen, col_count), jnp.bfloat16),
            pltpu.SemaphoreType.DMA((2,)),
        ],
        compiler_params=params,
        cost_estimate=pl.CostEstimate(flops=10**9, bytes_accessed=4 * 2**20, transcendentals=0),
        name="previous_group",
    )(halo, halo_other, own_value, mapped, value_weight, mid)


def solution(mesh):
    placed = (
        P(None, AXES, "grp"),
        P(None, AXES, None, "grp", None),
        P(None, AXES, None),
        P(None, "grp"),
        P(None, "grp"),
    )
    return jax.shard_map(
        shards,
        mesh=mesh,
        in_specs=placed,
        out_specs=P(None, AXES, "grp"),
        check_vma=False,
    )
```

time: 47.8 us -> 16.6 us (0.35); the launches traced: 47 us -> 16.5 us
  waiting for transfers between devices: 23 us -> 2.4 us
  matrix products: 8.11 us -> 0 us
  Pallas kernels: 0 us -> 8.1 us
  local copies, waits for them, and re-layouts: 5.01 us -> 0.02 us
  starting transfers between devices: 6.41 us -> 2.9 us
  other arithmetic: 1.15 us -> 0 us
    ppermute x2, waiting for transfers between devices: 23 us -> 2.4 us  [the longest x1 1.73 us: shards(): lax.ppermute(payload, AXES, [(i, (i + 1) % size) for i in range(size)])]
    dot_general x4 -> x0, matrix products: 8.11 us -> none  [the longest x1 4.9 us: attend_blocks(): jnp.einsum('bnhqk,bnkhd->bnqhd', attention, value_rows, preferred_element...]
    pallas_call x0 -> x4, Pallas kernels: none -> 8.1 us  [the longest x1 3.99 us: shards(): pl.pallas_call(local_kernel, out_shape=[jax.ShapeDtypeStruct((tok_count,...]
    ppermute x2, starting transfers between devices: 6.41 us -> 2.9 us  [the longest x1 1.55 us: shards(): halo_other = lax.ppermute(halo, 'grp', [(0, 1), (1, 0)])]
    unnamed x12 -> x8, local copies, waits for them, and re-layouts: 2.41 us -> 0.02 us
    convert_element_type x2 -> x0, local copies, waits for them, and re-layouts: 1.26 us -> none  [the longest x1 1.25 us: attend_blocks(): attended.astype(jnp.bfloat16)]
    slice x2 -> x0, local copies, waits for them, and re-layouts: 1.08 us -> none  [the longest x1 0.77 us: attend_padded(): return attended[:, 1:1 + tok_count]]
    sub x1 -> x0, other arithmetic: 0.48 us -> none  [attend_blocks(): weights = jnp.exp(scores - row_max)]
  transfers between devices with their start and end apart: 2 -> 2, of which waited for: 1 -> 2; matrix products, arithmetic and copies ran while one was open for 1% -> 0% of each run, Pallas kernels for 0% -> 27%
where the time goes in v1:
time: 16.6 us; the launch traced here: 16.5 us
  Pallas kernels  8.1 us (49%)
  blocking collectives  3.03 us (18%)
  starting transfers between devices  2.9 us (17%)
  waiting for transfers between devices  2.4 us (14%)
    pallas_call x1, Pallas kernels, shards(): pl.pallas_call(local_kernel, out_shape=[jax.ShapeDtypeStruct((tok_count,...  3.99 us
    all_gather x1, blocking collectives, shards(): enc = lax.all_gather(encodings, 'grp', axis=0)  3.03 us
    pallas_call x1, Pallas kernels, shards(): pl.pallas_call(halo_kernel, out_shape=jax.ShapeDtypeStruct(queries.shape,...  2.54 us
    ppermute x1, waiting for transfers between devices, shards(): lax.ppermute(payload, AXES, [(i, (i + 1) % size) for i in range(size)])  1.73 us
    ppermute x1, starting transfers between devices, shards(): halo_other = lax.ppermute(halo, 'grp', [(0, 1), (1, 0)])  1.55 us
    ppermute x1, starting transfers between devices, shards(): lax.ppermute(payload, AXES, [(i, (i + 1) % size) for i in range(size)])  1.35 us
    pallas_call x1, Pallas kernels, shards(): pl.pallas_call(payload_kernel, out_shape=[jax.ShapeDtypeStruct((neighbour...  1.13 us
    ppermute x1, waiting for transfers between devices, shards(): halo_other = lax.ppermute(halo, 'grp', [(0, 1), (1, 0)])  0.67 us
  transfers between devices with their start and end apart: 2, of which 2 were waited for; matrix products, arithmetic and copies ran while one was open for 0% of the time, Pallas kernels for 27%

profile of v1, /device:TPU:5, one launch (start us, length us, event | category | flops | bytes accessed | tf_op | source)
XLA Modules:
  0.0 16.5 jit_solution(14994307177366443053)
XLA Ops:
  0.0 0.0 copy-start.3
  0.0 0.0 copy-start
  0.0 0.0 copy-start.1
  0.0 0.0 copy-start.2
  0.0 1.1 %payload.1 = (bf16[2,64,896]{2,1,0:T(8,128)(2,1)S(1)}, s32[2,256]{1,0:T(2,128)S(1)}) custom-call(s32[1,2,2]{2,1,0:T(2,128)} %length_hbm.1, bf16[1,2,2,64,896]{4,3,2,1,0:T(8,128)(2,1)} %enc_hbm.1), custom_call_target="tpu_custom_call" | custom-call | flops 10000000000 | bytes 1048576 | tf_op jit(solution)/shard_map/payload/pallas_call | solution.py:169
  1.2 1.3 %collective-permute-start = (bf16[2,64,896]{2,1,0:T(8,128)(2,1)S(1)}, bf16[2,64,896]{2,1,0:T(8,128)(2,1)S(1)}, u32[]{:S(2)}, u32[]{:S(2)}) collective-permute-start(bf16[2,64,896]{2,1,0:T(8,128)(2,1)S(1)} %get-tuple-element.12), channel_id=1, source_target_pairs={{0,2},{2,4},{4,6},{6,8},{8,10},{10,12},{12,14},{14,16},{16,18},{18... | collective-permute-start | bytes 688136 | tf_op jit(solution)/shard_map/ppermute | solution.py:183
  2.5 0.0 copy-done.3
  2.5 3.0 %all-gather = bf16[2,2,2,64,896]{4,3,2,1,0:T(8,128)(2,1)S(1)} all-gather(bf16[1,2,2,64,896]{4,3,2,1,0:T(8,128)(2,1)S(1)} %copy-done.3), channel_id=2, replica_groups=mesh['seq'=4,'fsdp'=4,'grp'=2] {'grp'}, dimensions={0}, use_global_device_ids=true | all-gather | bytes 1376256 | tf_op jit(solution)/shard_map/all_gather | solution.py:184
  5.5 0.0 copy-done
  5.5 0.0 copy-done.1
  5.6 0.0 copy-done.2
  5.6 4.0 %local_groups.1 = (bf16[128,1024]{1,0:T(8,128)(2,1)S(1)}, bf16[512,896]{1,0:T(8,128)(2,1)S(1)}) custom-call(s32[2,256]{1,0:T(2,128)S(1)} %get-tuple-element.13.dead_ref, bf16[1,128,1024]{2,1,0:T(8,128)(2,1)S(1)} %copy-done.2, bf16[2,1,2,2,64,896]{5,4,3,2,1,0:T(8,128)(2,1)S(1)} %bitcast.1, bf16[896,1024]{1,0:T(8,128)(2,1)S(1)} %copy-done.1, ...), custom_call_target="tpu_custom_call" | custom-call | flops 2000000000 | bytes 6291456 | tf_op jit(solution)/shard_map/local_groups/pallas_call | solution.py:185
  9.6 1.7 %collective-permute-done.own_ref = bf16[2,64,896]{2,1,0:T(8,128)(2,1)S(1)} collective-permute-done((bf16[2,64,896]{2,1,0:T(8,128)(2,1)S(1)}, bf16[2,64,896]{2,1,0:T(8,128)(2,1)S(1)}, u32[]{:S(2)}, u32[]{:S(2)}) %collective-permute-start) | collective-permute-done | bytes 229408 | tf_op jit(solution)/shard_map/ppermute | solution.py:183
  11.3 1.5 %collective-permute-start.1 = (bf16[2,64,896]{2,1,0:T(8,128)(2,1)S(1)}, bf16[2,64,896]{2,1,0:T(8,128)(2,1)S(1)}, u32[]{:S(2)}, u32[]{:S(2)}) collective-permute-start(bf16[2,64,896]{2,1,0:T(8,128)(2,1)S(1)} %collective-permute-done.own_ref), channel_id=1, source_target_pairs={{0,1},{1,0},{2,3},{3,2},{4,5},{5,4},{6,7},{7,6},{8,9},{9,8},{10,11... | collective-permute-start | bytes 688136 | tf_op jit(solution)/shard_map/ppermute | solution.py:199
  12.8 0.4 %own_values.1.own_value_ref = bf16[128,1024]{1,0:T(8,128)(2,1)S(1)} custom-call(bf16[2,64,896]{2,1,0:T(8,128)(2,1)S(1)} %collective-permute-done.own_ref, bf16[896,1024]{1,0:T(8,128)(2,1)S(1)} %copy-done), custom_call_target="tpu_custom_call" | custom-call | flops 300000000 | bytes 1048576 | tf_op jit(solution)/shard_map/own_values/pallas_call | solution.py:200
  13.3 0.7 %collective-permute-done.1.other_ref = bf16[2,64,896]{2,1,0:T(8,128)(2,1)S(1)} collective-permute-done((bf16[2,64,896]{2,1,0:T(8,128)(2,1)S(1)}, bf16[2,64,896]{2,1,0:T(8,128)(2,1)S(1)}, u32[]{:S(2)}, u32[]{:S(2)}) %collective-permute-start.1) | collective-permute-done | bytes 229408 | tf_op jit(solution)/shard_map/ppermute | solution.py:199
  13.9 2.5 %previous_group.1 = bf16[1,128,1024]{2,1,0:T(8,128)(2,1)} custom-call(bf16[2,64,896]{2,1,0:T(8,128)(2,1)S(1)} %collective-permute-done.own_ref, bf16[2,64,896]{2,1,0:T(8,128)(2,1)S(1)} %collective-permute-done.1.other_ref, bf16[128,1024]{1,0:T(8,128)(2,1)S(1)} %own_values.1.own_value_ref, bf16[512,896]{1,0:T(8,128)(2,1)S(1)} %get-tuple-element.17.map_ref, ...), custom_call_target="tpu_custom_call" | custom-call | flops 1000000000 | bytes 4194304 | tf_op jit(solution)/shard_map/previous_group/pallas_call | solution.py:209
Async XLA Ops:
  0.0 2.5 %copy-start.3 = (bf16[1,2,2,64,896]{4,3,2,1,0:T(8,128)(2,1)S(1)}, bf16[1,2,2,64,896]{4,3,2,1,0:T(8,128)(2,1)}, u32[]{:S(2)}) copy-start(bf16[1,2,2,64,896]{4,3,2,1,0:T(8,128)(2,1)} %enc_hbm.1) | copy-start | bytes 1376260
  0.0 5.5 %copy-start = (bf16[896,1024]{1,0:T(8,128)(2,1)S(1)}, bf16[896,1024]{1,0:T(8,128)(2,1)}, u32[]{:S(2)}) copy-start(bf16[896,1024]{1,0:T(8,128)(2,1)} %vw_ref.5) | copy-start | bytes 5505028
  0.0 5.5 %copy-start.1 = (bf16[896,1024]{1,0:T(8,128)(2,1)S(1)}, bf16[896,1024]{1,0:T(8,128)(2,1)}, u32[]{:S(2)}) copy-start(bf16[896,1024]{1,0:T(8,128)(2,1)} %kw_ref.1) | copy-start | bytes 5505028
  0.0 5.5 %copy-start.2 = (bf16[1,128,1024]{2,1,0:T(8,128)(2,1)S(1)}, bf16[1,128,1024]{2,1,0:T(8,128)(2,1)}, u32[]{:S(2)}) copy-start(bf16[1,128,1024]{2,1,0:T(8,128)(2,1)} %query_ref.1) | copy-start | bytes 786436
  1.2 10.1 %collective-permute-start = (bf16[2,64,896]{2,1,0:T(8,128)(2,1)S(1)}, bf16[2,64,896]{2,1,0:T(8,128)(2,1)S(1)}, u32[]{:S(2)}, u32[]{:S(2)}) collective-permute-start(bf16[2,64,896]{2,1,0:T(8,128)(2,1)S(1)} %get-tuple-element.12), channel_id=1, source_target_pairs={{0,2},{2,4},{4,6},{6,8},{8,10},{10,12},{12,14},{14,16},{16,18},{18... | collective-permute-start | bytes 688136 | tf_op jit(solution)/shard_map/ppermute | solution.py:183
  11.3 2.7 %collective-permute-start.1 = (bf16[2,64,896]{2,1,0:T(8,128)(2,1)S(1)}, bf16[2,64,896]{2,1,0:T(8,128)(2,1)S(1)}, u32[]{:S(2)}, u32[]{:S(2)}) collective-permute-start(bf16[2,64,896]{2,1,0:T(8,128)(2,1)S(1)} %collective-permute-done.own_ref), channel_id=1, source_target_pairs={{0,1},{1,0},{2,3},{3,2},{4,5},{5,4},{6,7},{7,6},{8,9},{9,8},{10,11... | collective-permute-start | bytes 688136 | tf_op jit(solution)/shard_map/ppermute | solution.py:199

commit v2 on v1

v2 whole, which is shorter than its diff:
```python
import math

import jax
import jax.numpy as jnp
from jax import lax
from jax.experimental import pallas as pl
from jax.experimental.pallas import tpu as pltpu
from jax.sharding import PartitionSpec as P

HEAD_DIM = 128
MASK_FILL = -1e30
SCORE_SCALE = HEAD_DIM ** (-0.5) * math.log2(math.e)
DEAD = 8.0
AXES = ("seq", "fsdp")


def dot(a, b):
    return jnp.dot(a, b, preferred_element_type=jnp.float32)


def dot_nt(a, b):
    return lax.dot_general(a, b, (((1,), (1,)), ((), ())), preferred_element_type=jnp.float32)


def softmax_weights(scores, dead):
    scores = jnp.where(dead, MASK_FILL, scores)
    return jnp.exp2(scores - jnp.max(scores, axis=-1, keepdims=True)).astype(jnp.bfloat16)


def mix(weights, rows):
    ones = jnp.ones((rows.shape[0], 128), jnp.bfloat16)
    mixed = dot(weights, jnp.concatenate([rows, ones], axis=1))
    return mixed[:, :-128] * (1.0 / mixed[:, -1:])


def payload_kernel(length_hbm, enc_hbm, out_ref, length_ref, sems):
    group_count, neighbours, nb_half, _ = enc_hbm.shape[1:]
    copies = [
        pltpu.make_async_copy(length_hbm, length_ref, sems.at[0]),
        pltpu.make_async_copy(enc_hbm.at[0, group_count - 1], out_ref, sems.at[1]),
    ]
    for copy in copies:
        copy.start()
    row = lax.broadcasted_iota(jnp.int32, (nb_half, 128), 0) + lax.axis_index("grp") * nb_half
    lane = lax.broadcasted_iota(jnp.int32, (nb_half, 128), 1)
    copies[0].wait()
    marks = [(lane == 0) & (row >= length_ref[0, group_count - 1, n]) for n in range(neighbours)]
    copies[1].wait()
    for n in range(neighbours):
        part = out_ref[n, :, :128].astype(jnp.float32)
        out_ref[n, :, :128] = jnp.where(marks[n], DEAD, part).astype(jnp.bfloat16)


def local_kernel(length_ref, query_ref, enc_ref, kw_hbm, vw_hbm, out_ref, map_ref, vw_ref, kw_ref, sems):
    tok_count, col_count = query_ref.shape[1:]
    head_count = col_count // HEAD_DIM
    neighbours, nb_half, enc_width = enc_ref.shape[3:]
    half = neighbours * nb_half
    glen = tok_count // 2
    wide = 2 * HEAD_DIM
    copies = [
        [
            pltpu.make_async_copy(src.at[:, pl.ds(start, wide)], dst.at[:, pl.ds(start, wide)], sems.at[i, start // wide])
            for start in range(0, col_count, wide)
        ]
        for i, (src, dst) in enumerate([(kw_hbm, kw_ref), (vw_hbm, vw_ref)])
    ]
    for part in copies:
        for copy in part:
            copy.start()

    def group(g):
        rows = [enc_ref[core, 0, g].reshape(half, enc_width) for core in range(2)]
        key = lax.broadcasted_iota(jnp.int32, (1, 2 * half), 1)
        live = key < 0
        for block in range(2 * neighbours):
            first = block * nb_half
            length = jnp.broadcast_to(length_ref[0, g : g + 1, block % neighbours : block % neighbours + 1], key.shape)
            end = first + jnp.clip(length - block // neighbours * nb_half, 0, nb_half)
            live = live | ((key >= first) & (key < end))
        return jnp.concatenate(rows, axis=0), jnp.logical_not(live)

    query = query_ref[0].astype(jnp.float32)
    row = lax.broadcasted_iota(jnp.int32, (glen, 1), 0)
    halo_query = jnp.where(row < glen - 1, query[:glen], query[tok_count - 1 :]).astype(jnp.bfloat16)
    query = pltpu.roll(query, 1, 0)[glen:].astype(jnp.bfloat16)

    head_row = lax.broadcasted_iota(jnp.int32, (16, 1), 0)
    lane = lax.broadcasted_iota(jnp.int32, (1, enc_width), 1)
    one_hot = jnp.where(lane == 0, 1.0, 0.0)
    last = jnp.zeros((16, enc_width), jnp.float32)
    for h in range(head_count):
        cols = slice(h * HEAD_DIM, (h + 1) * HEAD_DIM)
        if h % 2 == 0:
            copies[0][h // 2].wait()
        mapped = dot_nt(halo_query[:, cols], kw_ref[:, cols]) * SCORE_SCALE
        last = jnp.where(head_row == h, mapped[glen - 1 :], last)
        map_ref[pl.ds(h * glen, glen), :] = jnp.where(row < glen - 1, mapped, one_hot).astype(jnp.bfloat16)

    enc, dead = group(1)
    last = mix(softmax_weights(dot_nt(last.astype(jnp.bfloat16), enc), dead), enc).astype(jnp.bfloat16)

    enc, dead = group(0)
    value_lhs = jnp.concatenate([enc, last], axis=0)
    for c in range(col_count // wide):
        cols = slice(c * wide, (c + 1) * wide)
        copies[1][c].wait()
        keys = dot(enc, kw_ref[:, cols]).astype(jnp.bfloat16)
        values = dot(value_lhs, vw_ref[:, cols])
        last_out = values[2 * half :]
        values = values[: 2 * half].astype(jnp.bfloat16)
        for i in range(2):
            h = 2 * c + i
            cols = slice(h * HEAD_DIM, (h + 1) * HEAD_DIM)
            own = slice(i * HEAD_DIM, (i + 1) * HEAD_DIM)
            weights = softmax_weights(dot_nt(query[:, cols], keys[:, own]) * SCORE_SCALE, dead)
            out = mix(weights, values[:, own])
            first = jnp.broadcast_to(last_out[h : h + 1, own], (glen, HEAD_DIM))
            out = pltpu.roll(jnp.concatenate([first, out], axis=0), tok_count - 1, 0)
            out_ref[:, cols] = out.astype(jnp.bfloat16)


def own_value_kernel(own_ref, vw_ref, value_ref):
    value_ref[...] = dot(own_ref[...].reshape(-1, own_ref.shape[-1]), vw_ref[...]).astype(jnp.bfloat16)


def halo_kernel(
    own_ref, other_ref, own_value_ref, map_ref, vw_ref, mid_ref, out_hbm, score_ref, max_ref, weight_ref, top_ref, sems
):
    tok_count, col_count = mid_ref.shape
    head_count = col_count // HEAD_DIM
    key_count = score_ref.shape[1]
    glen = tok_count // 2
    enc_width = own_ref.shape[-1]
    row = lax.broadcasted_iota(jnp.int32, (glen, 1), 0)
    is_first = lax.axis_index(AXES) == 0
    rest = pltpu.make_async_copy(mid_ref.at[pl.ds(glen, glen)], out_hbm.at[0, pl.ds(glen, glen)], sems.at[0])
    rest.start()

    @pl.when(is_first)
    def _():
        edge = mid_ref[:glen, :].astype(jnp.float32)
        top_ref[...] = jnp.where(row < glen - 1, 0.0, edge).astype(jnp.bfloat16)

    @pl.when(jnp.logical_not(is_first))
    def _():
        own, other = (ref[...].reshape(-1, enc_width) for ref in (own_ref, other_ref))
        score_ref[...] = dot_nt(map_ref[...], jnp.concatenate([own, other], axis=0))
        other_value = dot(other, vw_ref[...]).astype(jnp.bfloat16)
        dead = score_ref[glen - 1 : glen, :] > DEAD - 1.0
        blocks = [pl.ds(start, 32) for start in range(0, head_count * glen, 32)]
        for block in blocks:
            scores = jnp.where(dead, MASK_FILL, score_ref[block, :])
            max_ref[block, :] = jnp.broadcast_to(jnp.max(scores, axis=-1, keepdims=True), (32, 128))
        for block in blocks:
            top = max_ref[block, :]
            for start in range(0, key_count, 128):
                part = slice(start, start + 128)
                scores = jnp.where(dead[:, part], MASK_FILL, score_ref[block, part])
                weight_ref[block, part] = jnp.exp2(scores - top).astype(jnp.bfloat16)
        for h in range(head_count):
            cols = slice(h * HEAD_DIM, (h + 1) * HEAD_DIM)
            value = jnp.concatenate([own_value_ref[:, cols], other_value[:, cols]], axis=0)
            out = mix(weight_ref[pl.ds(h * glen, glen), :], value)
            out = jnp.where(row < glen - 1, out, mid_ref[:glen, cols].astype(jnp.float32))
            top_ref[:, cols] = out.astype(jnp.bfloat16)

    top = pltpu.make_async_copy(top_ref, out_hbm.at[0, pl.ds(0, glen)], sems.at[1])
    top.start()
    rest.wait()
    top.wait()


def shards(queries, encodings, neighbour_lengths, key_weight, value_weight):
    tok_count, col_count = queries.shape[1:]
    group_count, neighbours, nb_half, enc_width = encodings.shape[1:]
    key_count = 2 * neighbours * nb_half
    glen = tok_count // group_count
    rows = col_count // HEAD_DIM * glen
    vmem = pl.BlockSpec(memory_space=pltpu.VMEM)
    hbm = pl.BlockSpec(memory_space=pltpu.HBM)
    params = pltpu.CompilerParams(vmem_limit_bytes=24 * 2**20)

    payload = pl.pallas_call(
        payload_kernel,
        out_shape=jax.ShapeDtypeStruct((neighbours, nb_half, enc_width), jnp.bfloat16),
        in_specs=[hbm, hbm],
        out_specs=vmem,
        scratch_shapes=[pltpu.SMEM(neighbour_lengths.shape, jnp.int32), pltpu.SemaphoreType.DMA((2,))],
        compiler_params=pltpu.CompilerParams(vmem_limit_bytes=4 * 2**20),
        cost_estimate=pl.CostEstimate(flops=10**10, bytes_accessed=2**20, transcendentals=0),
        name="payload",
    )(*(pltpu.with_memory_space_constraint(x, pltpu.HBM) for x in (neighbour_lengths, encodings)))
    size = lax.axis_size(AXES)
    halo = lax.ppermute(payload, AXES, [(i, (i + 1) % size) for i in range(size)])
    enc = lax.all_gather(encodings, "grp", axis=0)
    key_weight, value_weight = (pltpu.with_memory_space_constraint(x, pltpu.HBM) for x in (key_weight, value_weight))
    mid, mapped, value_weight = pl.pallas_call(
        local_kernel,
        out_shape=[
            jax.ShapeDtypeStruct((tok_count, col_count), jnp.bfloat16),
            jax.ShapeDtypeStruct((rows, enc_width), jnp.bfloat16),
            jax.ShapeDtypeStruct(value_weight.shape, jnp.bfloat16),
        ],
        in_specs=[vmem] * 3 + [hbm] * 2,
        out_specs=[vmem] * 3,
        scratch_shapes=[
            pltpu.VMEM(key_weight.shape, jnp.bfloat16),
            pltpu.SemaphoreType.DMA((2, col_count // (2 * HEAD_DIM))),
        ],
        compiler_params=params,
        cost_estimate=pl.CostEstimate(flops=2 * 10**9, bytes_accessed=6 * 2**20, transcendentals=0),
        name="local_groups",
    )(neighbour_lengths, queries, enc, key_weight, value_weight)

    halo, mid, mapped = lax.optimization_barrier((halo, mid, mapped))
    halo_other = lax.ppermute(halo, "grp", [(0, 1), (1, 0)])
    own_value = pl.pallas_call(
        own_value_kernel,
        out_shape=jax.ShapeDtypeStruct((neighbours * nb_half, col_count), jnp.bfloat16),
        in_specs=[vmem] * 2,
        out_specs=vmem,
        compiler_params=params,
        cost_estimate=pl.CostEstimate(flops=3 * 10**8, bytes_accessed=2**20, transcendentals=0),
        name="own_values",
    )(halo, value_weight)
    return pl.pallas_call(
        halo_kernel,
        out_shape=jax.ShapeDtypeStruct(queries.shape, jnp.bfloat16),
        in_specs=[vmem] * 6,
        out_specs=hbm,
        scratch_shapes=[
            pltpu.VMEM((rows, key_count), jnp.float32),
            pltpu.VMEM((rows, 128), jnp.float32),
            pltpu.VMEM((rows, key_count), jnp.bfloat16),
            pltpu.VMEM((glen, col_count), jnp.bfloat16),
            pltpu.SemaphoreType.DMA((2,)),
        ],
        compiler_params=params,
        cost_estimate=pl.CostEstimate(flops=10**9, bytes_accessed=4 * 2**20, transcendentals=0),
        name="previous_group",
    )(halo, halo_other, own_value, mapped, value_weight, mid)


def solution(mesh):
    placed = (
        P(None, AXES, "grp"),
        P(None, AXES, None, "grp", None),
        P(None, AXES, None),
        P(None, "grp"),
        P(None, "grp"),
    )
    return jax.shard_map(
        shards,
        mesh=mesh,
        in_specs=placed,
        out_specs=P(None, AXES, "grp"),
        check_vma=False,
    )
```

time: 16.6 us -> 16 us (0.964)
  the two profiles are of different devices: /device:TPU:5 before, /device:TPU:0 now
where the time goes in v2:
time: 16 us; the launch traced here: 15.8 us
  Pallas kernels  8.92 us (56%)
  starting transfers between devices  3.08 us (19%)
  blocking collectives  2.45 us (15%)
  waiting for transfers between devices  1.36 us (8%)
    pallas_call x1, Pallas kernels, shards(): pl.pallas_call(local_kernel, out_shape=[jax.ShapeDtypeStruct((tok_count,...  6.71 us
    ppermute x1, starting transfers between devices, shards(): lax.ppermute(payload, AXES, [(i, (i + 1) % size) for i in range(size)])  3.08 us
    all_gather x1, blocking collectives, shards(): enc = lax.all_gather(encodings, 'grp', axis=0)  2.45 us
    pallas_call x1, Pallas kernels, shards(): pl.pallas_call(payload_kernel, out_shape=jax.ShapeDtypeStruct((neighbours...  1.04 us
    ppermute x1, waiting for transfers between devices, shards(): halo_other = lax.ppermute(halo, 'grp', [(0, 1), (1, 0)])  1.03 us
    pallas_call x1, Pallas kernels, shards(): pl.pallas_call(halo_kernel, out_shape=jax.ShapeDtypeStruct(queries.shape,...  0.72 us
    pallas_call x1, Pallas kernels, shards(): pl.pallas_call(own_value_kernel, out_shape=jax.ShapeDtypeStruct((neighbou...  0.45 us
    ppermute x1, waiting for transfers between devices, shards(): lax.ppermute(payload, AXES, [(i, (i + 1) % size) for i in range(size)])  0.33 us
  transfers between devices with their start and end apart: 2, of which 2 were waited for; matrix products, arithmetic and copies ran while one was open for 0% of the time, Pallas kernels for 45%

profile of v2, /device:TPU:0, one launch (start us, length us, event | category | flops | bytes accessed | tf_op | source)
XLA Modules:
  0.0 15.8 jit_solution(13190135696414996727)
XLA Ops:
  0.0 0.0 copy-start.2
  0.0 0.0 copy-start.1
  0.0 0.0 copy-start
  0.0 1.0 %payload.1 = bf16[2,64,896]{2,1,0:T(8,128)(2,1)S(1)} custom-call(s32[1,2,2]{2,1,0:T(2,128)} %length_ref.1, bf16[1,2,2,64,896]{4,3,2,1,0:T(8,128)(2,1)} %enc_hbm.1), custom_call_target="tpu_custom_call" | custom-call | flops 10000000000 | bytes 1048576 | tf_op jit(solution)/shard_map/payload/pallas_call | solution.py:184
  1.1 3.1 %collective-permute-start = (bf16[2,64,896]{2,1,0:T(8,128)(2,1)S(1)}, bf16[2,64,896]{2,1,0:T(8,128)(2,1)S(1)}, u32[]{:S(2)}, u32[]{:S(2)}) collective-permute-start(bf16[2,64,896]{2,1,0:T(8,128)(2,1)S(1)} %payload.1), channel_id=1, source_target_pairs={{0,2},{2,4},{4,6},{6,8},{8,10},{10,12},{12,14},{14,16},{16,18},{18... | collective-permute-start | bytes 688136 | tf_op jit(solution)/shard_map/ppermute | solution.py:195
  4.1 0.0 copy-done.2
  4.1 2.5 %all-gather = bf16[2,2,2,64,896]{4,3,2,1,0:T(8,128)(2,1)S(1)} all-gather(bf16[1,2,2,64,896]{4,3,2,1,0:T(8,128)(2,1)S(1)} %copy-done.2), channel_id=2, replica_groups=mesh['seq'=4,'fsdp'=4,'grp'=2] {'grp'}, dimensions={0}, use_global_device_ids=true | all-gather | bytes 1376256 | tf_op jit(solution)/shard_map/all_gather | solution.py:196
  6.6 0.0 copy-done.1
  6.6 0.0 copy-done
  6.6 6.7 %local_groups.1 = (bf16[128,1024]{1,0:T(8,128)(2,1)S(1)}, bf16[512,896]{1,0:T(8,128)(2,1)S(1)}, bf16[896,1024]{1,0:T(8,128)(2,1)S(1)}) custom-call(s32[1,2,2]{2,1,0:T(2,128)S(1)} %copy-done.1, bf16[1,128,1024]{2,1,0:T(8,128)(2,1)S(1)} %copy-done, bf16[2,1,2,2,64,896]{5,4,3,2,1,0:T(8,128)(2,1)S(1)} %bitcast.1, bf16[896,1024]{1,0:T(8,128)(2,1)} %kw_hbm.1, ...), custom_call_target="tpu_custom_call" | custom-call | flops 2000000000 | bytes 6291456 | tf_op jit(solution)/shard_map/local_groups/pallas_call | solution.py:198
  13.3 0.3 %collective-permute-done.own_ref = bf16[2,64,896]{2,1,0:T(8,128)(2,1)S(1)} collective-permute-done((bf16[2,64,896]{2,1,0:T(8,128)(2,1)S(1)}, bf16[2,64,896]{2,1,0:T(8,128)(2,1)S(1)}, u32[]{:S(2)}, u32[]{:S(2)}) %collective-permute-start) | collective-permute-done | bytes 229408 | tf_op jit(solution)/shard_map/ppermute | solution.py:195
  13.6 0.0 collective-permute-start.1
  13.6 0.5 %own_values.1.own_value_ref = bf16[128,1024]{1,0:T(8,128)(2,1)S(1)} custom-call(bf16[2,64,896]{2,1,0:T(8,128)(2,1)S(1)} %collective-permute-done.own_ref, bf16[896,1024]{1,0:T(8,128)(2,1)S(1)} %get-tuple-element.14.vw_ref), custom_call_target="tpu_custom_call" | custom-call | flops 300000000 | bytes 1048576 | tf_op jit(solution)/shard_map/own_values/pallas_call | solution.py:218
  14.1 1.0 %collective-permute-done.1.other_ref = bf16[2,64,896]{2,1,0:T(8,128)(2,1)S(1)} collective-permute-done((bf16[2,64,896]{2,1,0:T(8,128)(2,1)S(1)}, bf16[2,64,896]{2,1,0:T(8,128)(2,1)S(1)}, u32[]{:S(2)}, u32[]{:S(2)}) %collective-permute-start.1) | collective-permute-done | bytes 229408 | tf_op jit(solution)/shard_map/ppermute | solution.py:217
  15.1 0.7 %previous_group.1 = bf16[1,128,1024]{2,1,0:T(8,128)(2,1)} custom-call(bf16[2,64,896]{2,1,0:T(8,128)(2,1)S(1)} %collective-permute-done.own_ref, bf16[2,64,896]{2,1,0:T(8,128)(2,1)S(1)} %collective-permute-done.1.other_ref, bf16[128,1024]{1,0:T(8,128)(2,1)S(1)} %own_values.1.own_value_ref, bf16[512,896]{1,0:T(8,128)(2,1)S(1)} %get-tuple-element.15.map_ref, ...), custom_call_target="tpu_custom_call" | custom-call | flops 1000000000 | bytes 4194304 | tf_op jit(solution)/shard_map/previous_group/pallas_call | solution.py:227
Async XLA Ops:
  0.0 4.1 %copy-start.2 = (bf16[1,2,2,64,896]{4,3,2,1,0:T(8,128)(2,1)S(1)}, bf16[1,2,2,64,896]{4,3,2,1,0:T(8,128)(2,1)}, u32[]{:S(2)}) copy-start(bf16[1,2,2,64,896]{4,3,2,1,0:T(8,128)(2,1)} %enc_hbm.1) | copy-start | bytes 1376260
  0.0 6.6 %copy-start.1 = (s32[1,2,2]{2,1,0:T(2,128)S(1)}, s32[1,2,2]{2,1,0:T(2,128)}, u32[]{:S(2)}) copy-start(s32[1,2,2]{2,1,0:T(2,128)} %length_ref.1) | copy-start | bytes 52
  0.0 6.6 %copy-start = (bf16[1,128,1024]{2,1,0:T(8,128)(2,1)S(1)}, bf16[1,128,1024]{2,1,0:T(8,128)(2,1)}, u32[]{:S(2)}) copy-start(bf16[1,128,1024]{2,1,0:T(8,128)(2,1)} %query_ref.1) | copy-start | bytes 786436
  1.1 12.6 %collective-permute-start = (bf16[2,64,896]{2,1,0:T(8,128)(2,1)S(1)}, bf16[2,64,896]{2,1,0:T(8,128)(2,1)S(1)}, u32[]{:S(2)}, u32[]{:S(2)}) collective-permute-start(bf16[2,64,896]{2,1,0:T(8,128)(2,1)S(1)} %payload.1), channel_id=1, source_target_pairs={{0,2},{2,4},{4,6},{6,8},{8,10},{10,12},{12,14},{14,16},{16,18},{18... | collective-permute-start | bytes 688136 | tf_op jit(solution)/shard_map/ppermute | solution.py:195
  13.6 1.5 %collective-permute-start.1 = (bf16[2,64,896]{2,1,0:T(8,128)(2,1)S(1)}, bf16[2,64,896]{2,1,0:T(8,128)(2,1)S(1)}, u32[]{:S(2)}, u32[]{:S(2)}) collective-permute-start(bf16[2,64,896]{2,1,0:T(8,128)(2,1)S(1)} %collective-permute-done.own_ref), channel_id=1, source_target_pairs={{0,1},{1,0},{2,3},{3,2},{4,5},{5,4},{6,7},{7,6},{8,9},{9,8},{10,11... | collective-permute-start | bytes 688136 | tf_op jit(solution)/shard_map/ppermute | solution.py:217

commit v3 on v2

v3 whole, which is shorter than its diff:
```python
import functools
import math

import jax
import jax.numpy as jnp
from jax import lax
from jax.experimental import pallas as pl
from jax.experimental.pallas import tpu as pltpu
from jax.sharding import PartitionSpec as P

HEAD_DIM = 128
MASK_FILL = -1e30
SCORE_SCALE = HEAD_DIM ** (-0.5) * math.log2(math.e)
DEAD = 8.0
AXES = ("seq", "fsdp")


def dot(a, b):
    return jnp.dot(a, b, preferred_element_type=jnp.float32)


def dot_nt(a, b):
    return lax.dot_general(a, b, (((1,), (1,)), ((), ())), preferred_element_type=jnp.float32)


def softmax_weights(scores, dead):
    scores = jnp.where(dead, MASK_FILL, scores)
    return jnp.exp2(scores - jnp.max(scores, axis=-1, keepdims=True)).astype(jnp.bfloat16)


def mix(weights, rows):
    ones = jnp.ones((rows.shape[0], 128), jnp.bfloat16)
    mixed = dot(weights, jnp.concatenate([rows, ones], axis=1))
    return mixed[:, :-128] * (1.0 / mixed[:, -1:])


def payload_kernel(length_hbm, enc_hbm, out_ref, length_ref, sems):
    group_count, neighbours, nb_half, _ = enc_hbm.shape[1:]
    quarters = [(n, pl.ds(i * nb_half // 2, nb_half // 2)) for n in range(neighbours) for i in range(2)]
    copies = [
        pltpu.make_async_copy(enc_hbm.at[0, group_count - 1].at[part], out_ref.at[part], sems.at[i])
        for i, part in enumerate(quarters)
    ]
    lengths = pltpu.make_async_copy(length_hbm, length_ref, sems.at[len(copies)])
    lengths.start()
    for copy in copies:
        copy.start()
    row = lax.broadcasted_iota(jnp.int32, (nb_half, 128), 0) + lax.axis_index("grp") * nb_half
    lane = lax.broadcasted_iota(jnp.int32, (nb_half, 128), 1)
    lengths.wait()
    marks = [(lane == 0) & (row >= length_ref[0, group_count - 1, n]) for n in range(neighbours)]
    for copy in copies:
        copy.wait()
    for n in range(neighbours):
        part = out_ref[n, :, :128].astype(jnp.float32)
        out_ref[n, :, :128] = jnp.where(marks[n], DEAD, part).astype(jnp.bfloat16)


def local_kernel(
    length_ref, query_ref, enc_ref, kw_hbm, vw_hbm, out_hbm, edge_ref, map_ref, vw_ref,
    kw_ref, key_ref, value_ref, score_ref, max_ref, weight_ref, out_ref, sems,
):
    tok_count, col_count = query_ref.shape[1:]
    head_count = col_count // HEAD_DIM
    neighbours, nb_half, enc_width = enc_ref.shape[3:]
    half = neighbours * nb_half
    glen = tok_count // 2
    heads = [slice(start, start + HEAD_DIM) for start in range(0, col_count, HEAD_DIM)]

    parts = sems.shape[1]
    depth = enc_width // parts
    copies = [
        [
            pltpu.make_async_copy(src.at[pl.ds(i * depth, depth)], dst.at[pl.ds(i * depth, depth)], sems.at[j, i])
            for i in range(parts)
        ]
        for j, (src, dst) in enumerate([(kw_hbm, kw_ref), (vw_hbm, vw_ref)])
    ]
    for weight_copies in copies:
        for copy in weight_copies:
            copy.start()

    def group(g):
        rows = [enc_ref[core, 0, g].reshape(half, enc_width) for core in range(2)]
        key = lax.broadcasted_iota(jnp.int32, (1, 2 * half), 1)
        live = key < 0
        for block in range(2 * neighbours):
            first = block * nb_half
            length = jnp.broadcast_to(length_ref[0, g : g + 1, block % neighbours : block % neighbours + 1], key.shape)
            end = first + jnp.clip(length - block // neighbours * nb_half, 0, nb_half)
            live = live | ((key >= first) & (key < end))
        return jnp.concatenate(rows, axis=0), jnp.logical_not(live)

    query = query_ref[0].astype(jnp.float32)
    row = lax.broadcasted_iota(jnp.int32, (glen, 1), 0)
    halo_query = jnp.where(row < glen - 1, query[:glen], query[tok_count - 1 :]).astype(jnp.bfloat16)
    query = pltpu.roll(query, 1, 0)[glen:].astype(jnp.bfloat16)

    enc, dead = group(0)
    for copy in copies[0]:
        copy.wait()
    key_ref[...] = dot(enc, kw_ref[...]).astype(jnp.bfloat16)

    head_row = lax.broadcasted_iota(jnp.int32, (16, 1), 0)
    lane = lax.broadcasted_iota(jnp.int32, (1, enc_width), 1)
    one_hot = jnp.where(lane == 0, 1.0, 0.0)
    last = jnp.zeros((16, enc_width), jnp.float32)
    for h, cols in enumerate(heads):
        mapped = dot_nt(halo_query[:, cols], kw_ref[:, cols]) * SCORE_SCALE
        last = jnp.where(head_row == h, mapped[glen - 1 :], last)
        map_ref[pl.ds(h * glen, glen), :] = jnp.where(row < glen - 1, mapped, one_hot).astype(jnp.bfloat16)
    for h, cols in enumerate(heads):
        score_ref[pl.ds(h * glen, glen), :] = dot_nt(query[:, cols], key_ref[:, cols]) * SCORE_SCALE

    last_enc, last_dead = group(1)
    last_weights = softmax_weights(dot_nt(last.astype(jnp.bfloat16), last_enc), last_dead)
    last = mix(last_weights, last_enc).astype(jnp.bfloat16)

    blocks = [pl.ds(start, 32) for start in range(0, head_count * glen, 32)]
    for block in blocks:
        scores = jnp.where(dead, MASK_FILL, score_ref[block, :])
        max_ref[block, :] = jnp.broadcast_to(jnp.max(scores, axis=-1, keepdims=True), (32, 128))
    for block in blocks:
        top = max_ref[block, :]
        for start in range(0, 2 * half, 128):
            part = slice(start, start + 128)
            scores = jnp.where(dead[:, part], MASK_FILL, score_ref[block, part])
            weight_ref[block, part] = jnp.exp2(scores - top).astype(jnp.bfloat16)

    for copy in copies[1]:
        copy.wait()
    values = dot(jnp.concatenate([enc, last], axis=0), vw_ref[...])
    value_ref[...] = values[: 2 * half].astype(jnp.bfloat16)
    last_out = values[2 * half :]
    token = lax.broadcasted_iota(jnp.int32, (tok_count, 1), 0)
    for h, cols in enumerate(heads):
        out = mix(weight_ref[pl.ds(h * glen, glen), :], value_ref[:, cols])
        first = jnp.broadcast_to(last_out[h : h + 1, cols], (glen, HEAD_DIM))
        out = pltpu.roll(jnp.concatenate([first, out], axis=0), tok_count - 1, 0)
        edge_ref[:, cols] = out[glen - 1 : glen]
        out_ref[:, cols] = jnp.where(token < glen - 1, 0.0, out).astype(jnp.bfloat16)
    copy = pltpu.make_async_copy(out_ref, out_hbm.at[0], sems.at[0, 0])
    copy.start()
    copy.wait()


def own_kernel(glen, own_ref, map_ref, vw_ref, value_ref, score_ref, max_ref):
    own = own_ref[...].reshape(-1, own_ref.shape[-1])
    value_ref[...] = dot(own, vw_ref[...]).astype(jnp.bfloat16)
    score_ref[...] = dot_nt(map_ref[...], own)
    dead = score_ref[glen - 1 : glen, :] > DEAD - 1.0
    for start in range(0, score_ref.shape[0], 32):
        block = pl.ds(start, 32)
        scores = jnp.where(dead, MASK_FILL, score_ref[block, :])
        score_ref[block, :] = scores
        max_ref[block, :] = jnp.broadcast_to(jnp.max(scores, axis=-1, keepdims=True), scores.shape)


def halo_kernel(
    other_ref, own_value_ref, own_score_ref, own_max_ref, map_ref, vw_ref, edge_ref, _, out_hbm,
    score_ref, max_ref, weight_ref, top_ref, sem,
):
    glen, col_count = top_ref.shape
    row_count, half = score_ref.shape

    @pl.when(lax.axis_index(AXES) > 0)
    def _():
        other = other_ref[...].reshape(half, -1)
        score_ref[...] = dot_nt(map_ref[...], other)
        other_value = dot(other, vw_ref[...]).astype(jnp.bfloat16)
        dead = score_ref[glen - 1 : glen, :] > DEAD - 1.0
        blocks = [pl.ds(start, 32) for start in range(0, row_count, 32)]
        for block in blocks:
            scores = jnp.where(dead, MASK_FILL, score_ref[block, :])
            own_max = own_max_ref[block, :]
            max_ref[block, :] = jnp.maximum(own_max, jnp.max(scores, axis=-1, keepdims=True))
        for block in blocks:
            top = max_ref[block, :]
            weight_ref[block, :half] = jnp.exp2(own_score_ref[block, :] - top).astype(jnp.bfloat16)
            scores = jnp.where(dead, MASK_FILL, score_ref[block, :])
            weight_ref[block, half:] = jnp.exp2(scores - top).astype(jnp.bfloat16)
        row = lax.broadcasted_iota(jnp.int32, (glen, 1), 0)
        for start in range(0, col_count, HEAD_DIM):
            cols = slice(start, start + HEAD_DIM)
            value = jnp.concatenate([own_value_ref[:, cols], other_value[:, cols]], axis=0)
            out = mix(weight_ref[pl.ds(start // HEAD_DIM * glen, glen), :], value)
            top_ref[:, cols] = jnp.where(row < glen - 1, out, edge_ref[:, cols]).astype(jnp.bfloat16)
        copy = pltpu.make_async_copy(top_ref, out_hbm.at[0, pl.ds(0, glen)], sem)
        copy.start()
        copy.wait()


def shards(queries, encodings, neighbour_lengths, key_weight, value_weight):
    tok_count, col_count = queries.shape[1:]
    group_count, neighbours, nb_half, enc_width = encodings.shape[1:]
    half = neighbours * nb_half
    glen = tok_count // group_count
    rows = col_count // HEAD_DIM * glen
    vmem = pl.BlockSpec(memory_space=pltpu.VMEM)
    hbm = pl.BlockSpec(memory_space=pltpu.HBM)
    params = pltpu.CompilerParams(vmem_limit_bytes=24 * 2**20)

    payload = pl.pallas_call(
        payload_kernel,
        out_shape=jax.ShapeDtypeStruct((neighbours, nb_half, enc_width), jnp.bfloat16),
        in_specs=[hbm, hbm],
        out_specs=vmem,
        scratch_shapes=[pltpu.SMEM(neighbour_lengths.shape, jnp.int32), pltpu.SemaphoreType.DMA((2 * neighbours + 1,))],
        compiler_params=pltpu.CompilerParams(vmem_limit_bytes=4 * 2**20),
        cost_estimate=pl.CostEstimate(flops=10**10, bytes_accessed=2**20, transcendentals=0),
        name="payload",
    )(*(pltpu.with_memory_space_constraint(x, pltpu.HBM) for x in (neighbour_lengths, encodings)))
    size = lax.axis_size(AXES)
    halo = lax.ppermute(payload, AXES, [(i, (i + 1) % size) for i in range(size)])
    enc = lax.all_gather(encodings, "grp", axis=0)
    key_weight, value_weight = (pltpu.with_memory_space_constraint(x, pltpu.HBM) for x in (key_weight, value_weight))
    out, edge, mapped, value_weight = pl.pallas_call(
        local_kernel,
        out_shape=[
            jax.ShapeDtypeStruct(queries.shape, jnp.bfloat16),
            jax.ShapeDtypeStruct((1, col_count), jnp.float32),
            jax.ShapeDtypeStruct((rows, enc_width), jnp.bfloat16),
            jax.ShapeDtypeStruct(value_weight.shape, jnp.bfloat16),
        ],
        in_specs=[vmem] * 3 + [hbm] * 2,
        out_specs=[hbm] + [vmem] * 3,
        scratch_shapes=[
            pltpu.VMEM(key_weight.shape, jnp.bfloat16),
            pltpu.VMEM((2 * half, col_count), jnp.bfloat16),
            pltpu.VMEM((2 * half, col_count), jnp.bfloat16),
            pltpu.VMEM((rows, 2 * half), jnp.float32),
            pltpu.VMEM((rows, 128), jnp.float32),
            pltpu.VMEM((rows, 2 * half), jnp.bfloat16),
            pltpu.VMEM((tok_count, col_count), jnp.bfloat16),
            pltpu.SemaphoreType.DMA((2, 4)),
        ],
        compiler_params=params,
        cost_estimate=pl.CostEstimate(flops=2 * 10**9, bytes_accessed=6 * 2**20, transcendentals=0),
        name="local_groups",
    )(neighbour_lengths, queries, enc, key_weight, value_weight)

    halo, out, mapped = lax.optimization_barrier((halo, out, mapped))
    halo_other = lax.ppermute(halo, "grp", [(0, 1), (1, 0)])
    own_value, own_score, own_max = pl.pallas_call(
        functools.partial(own_kernel, glen),
        out_shape=[
            jax.ShapeDtypeStruct((half, col_count), jnp.bfloat16),
            jax.ShapeDtypeStruct((rows, half), jnp.float32),
            jax.ShapeDtypeStruct((rows, half), jnp.float32),
        ],
        in_specs=[vmem] * 3,
        out_specs=[vmem] * 3,
        compiler_params=params,
        cost_estimate=pl.CostEstimate(flops=3 * 10**8, bytes_accessed=2**20, transcendentals=0),
        name="own_half",
    )(halo, mapped, value_weight)
    return pl.pallas_call(
        halo_kernel,
        out_shape=jax.ShapeDtypeStruct(queries.shape, jnp.bfloat16),
        in_specs=[vmem] * 7 + [hbm],
        out_specs=hbm,
        scratch_shapes=[
            pltpu.VMEM((rows, half), jnp.float32),
            pltpu.VMEM((rows, half), jnp.float32),
            pltpu.VMEM((rows, 2 * half), jnp.bfloat16),
            pltpu.VMEM((glen, col_count), jnp.bfloat16),
            pltpu.SemaphoreType.DMA,
        ],
        input_output_aliases={7: 0},
        compiler_params=params,
        cost_estimate=pl.CostEstimate(flops=10**9, bytes_accessed=4 * 2**20, transcendentals=0),
        name="previous_group",
    )(
        halo_other, own_value, own_score, own_max, mapped, value_weight, edge,
        pltpu.with_memory_space_constraint(out, pltpu.HBM),
    )


def solution(mesh):
    placed = (
        P(None, AXES, "grp"),
        P(None, AXES, None, "grp", None),
        P(None, AXES, None),
        P(None, "grp"),
        P(None, "grp"),
    )
    return jax.shard_map(
        shards,
        mesh=mesh,
        in_specs=placed,
        out_specs=P(None, AXES, "grp"),
        check_vma=False,
    )
```

time: 16 us -> 15.6 us (0.975)
  the two profiles are of different devices: /device:TPU:0 before, /device:TPU:5 now
where the time goes in v3:
time: 15.6 us; the launch traced here: 15.5 us
  Pallas kernels  8.68 us (56%)
  blocking collectives  3.03 us (19%)
  starting transfers between devices  2.9 us (19%)
  waiting for transfers between devices  0.83 us (5%)
    pallas_call x1, Pallas kernels, shards(): pl.pallas_call(local_kernel, out_shape=[jax.ShapeDtypeStruct(queries.shap...  5.23 us
    all_gather x1, blocking collectives, shards(): enc = lax.all_gather(encodings, 'grp', axis=0)  3.03 us
    pallas_call x1, Pallas kernels, shards(): pl.pallas_call(halo_kernel, out_shape=jax.ShapeDtypeStruct(queries.shape,...  1.64 us
    ppermute x1, starting transfers between devices, shards(): halo_other = lax.ppermute(halo, 'grp', [(0, 1), (1, 0)])  1.55 us
    ppermute x1, starting transfers between devices, shards(): lax.ppermute(payload, AXES, [(i, (i + 1) % size) for i in range(size)])  1.35 us
    pallas_call x1, Pallas kernels, shards(): pl.pallas_call(payload_kernel, out_shape=jax.ShapeDtypeStruct((neighbours...  1.03 us
    pallas_call x1, Pallas kernels, shards(): pl.pallas_call(functools.partial(own_kernel, glen), out_shape=[jax.ShapeD...  0.78 us
    ppermute x1, waiting for transfers between devices, shards(): lax.ppermute(payload, AXES, [(i, (i + 1) % size) for i in range(size)])  0.49 us
  transfers between devices with their start and end apart: 2, of which 2 were waited for; matrix products, arithmetic and copies ran while one was open for 0% of the time, Pallas kernels for 39%

profile of v3, /device:TPU:5, one launch (start us, length us, event | category | flops | bytes accessed | tf_op | source)
XLA Modules:
  0.0 15.5 jit_solution(5042764136493216570)
XLA Ops:
  0.0 0.0 copy-start.1
  0.0 0.0 copy-start.2
  0.0 0.0 copy-start
  0.0 1.0 %payload.1 = bf16[2,64,896]{2,1,0:T(8,128)(2,1)S(1)} custom-call(s32[1,2,2]{2,1,0:T(2,128)} %length_ref.1, bf16[1,2,2,64,896]{4,3,2,1,0:T(8,128)(2,1)} %enc_hbm.1), custom_call_target="tpu_custom_call" | custom-call | flops 10000000000 | bytes 1048576 | tf_op jit(solution)/shard_map/payload/pallas_call | solution.py:203
  1.0 1.3 %collective-permute-start = (bf16[2,64,896]{2,1,0:T(8,128)(2,1)S(1)}, bf16[2,64,896]{2,1,0:T(8,128)(2,1)S(1)}, u32[]{:S(2)}, u32[]{:S(2)}) collective-permute-start(bf16[2,64,896]{2,1,0:T(8,128)(2,1)S(1)} %payload.1), channel_id=1, source_target_pairs={{0,2},{2,4},{4,6},{6,8},{8,10},{10,12},{12,14},{14,16},{16,18},{18... | collective-permute-start | bytes 688136 | tf_op jit(solution)/shard_map/ppermute | solution.py:214
  2.4 0.0 copy-done.2
  2.4 3.0 %all-gather = bf16[2,2,2,64,896]{4,3,2,1,0:T(8,128)(2,1)S(1)} all-gather(bf16[1,2,2,64,896]{4,3,2,1,0:T(8,128)(2,1)S(1)} %copy-done.2), channel_id=2, replica_groups=mesh['seq'=4,'fsdp'=4,'grp'=2] {'grp'}, dimensions={0}, use_global_device_ids=true | all-gather | bytes 1376256 | tf_op jit(solution)/shard_map/all_gather | solution.py:215
  5.4 0.0 copy-done.1
  5.4 0.0 copy-done
  5.4 5.2 %local_groups.1 = (bf16[1,128,1024]{2,1,0:T(8,128)(2,1)}, f32[1,1024]{1,0:T(1,128)S(1)}, bf16[512,896]{1,0:T(8,128)(2,1)S(1)}, bf16[896,1024]{1,0:T(8,128)(2,1)S(1)}) custom-call(s32[1,2,2]{2,1,0:T(2,128)S(1)} %copy-done.1, bf16[1,128,1024]{2,1,0:T(8,128)(2,1)S(1)} %copy-done, bf16[2,1,2,2,64,896]{5,4,3,2,1,0:T(8,128)(2,1)S(1)} %bitcast.1, ...), custom_call_target="tpu_custom_call" | custom-call | flops 2000000000 | bytes 6291456 | tf_op jit(solution)/shard_map/local_groups/pallas_call | solution.py:217
  10.7 0.5 %collective-permute-done.own_ref = bf16[2,64,896]{2,1,0:T(8,128)(2,1)S(1)} collective-permute-done((bf16[2,64,896]{2,1,0:T(8,128)(2,1)S(1)}, bf16[2,64,896]{2,1,0:T(8,128)(2,1)S(1)}, u32[]{:S(2)}, u32[]{:S(2)}) %collective-permute-start) | collective-permute-done | bytes 229408 | tf_op jit(solution)/shard_map/ppermute | solution.py:214
  11.2 1.5 %collective-permute-start.1 = (bf16[2,64,896]{2,1,0:T(8,128)(2,1)S(1)}, bf16[2,64,896]{2,1,0:T(8,128)(2,1)S(1)}, u32[]{:S(2)}, u32[]{:S(2)}) collective-permute-start(bf16[2,64,896]{2,1,0:T(8,128)(2,1)S(1)} %collective-permute-done.own_ref), channel_id=1, source_target_pairs={{0,1},{1,0},{2,3},{3,2},{4,5},{5,4},{6,7},{7,6},{8,9},{9,8},{10,11... | collective-permute-start | bytes 688136 | tf_op jit(solution)/shard_map/ppermute | solution.py:243
  12.7 0.8 %own_half.1 = (bf16[128,1024]{1,0:T(8,128)(2,1)S(1)}, f32[512,128]{1,0:T(8,128)S(1)}, f32[512,128]{1,0:T(8,128)S(1)}) custom-call(bf16[2,64,896]{2,1,0:T(8,128)(2,1)S(1)} %collective-permute-done.own_ref, bf16[512,896]{1,0:T(8,128)(2,1)S(1)} %get-tuple-element.18.map_ref, bf16[896,1024]{1,0:T(8,128)(2,1)S(1)} %get-tuple-element.19.vw_ref), custom_call_target="tpu_custom_call" | custom-call | flops 300000000 | bytes 1048576 | tf_op jit(solution)/shard_map/own_half/pallas_call | solution.py:244
  13.5 0.3 %collective-permute-done.1.other_ref = bf16[2,64,896]{2,1,0:T(8,128)(2,1)S(1)} collective-permute-done((bf16[2,64,896]{2,1,0:T(8,128)(2,1)S(1)}, bf16[2,64,896]{2,1,0:T(8,128)(2,1)S(1)}, u32[]{:S(2)}, u32[]{:S(2)}) %collective-permute-start.1) | collective-permute-done | bytes 229408 | tf_op jit(solution)/shard_map/ppermute | solution.py:243
  13.8 1.6 %previous_group.1 = bf16[1,128,1024]{2,1,0:T(8,128)(2,1)} custom-call(bf16[2,64,896]{2,1,0:T(8,128)(2,1)S(1)} %collective-permute-done.1.other_ref, bf16[128,1024]{1,0:T(8,128)(2,1)S(1)} %get-tuple-element.20.own_value_ref, f32[512,128]{1,0:T(8,128)S(1)} %get-tuple-element.21.own_score_ref, ...), custom_call_target="tpu_custom_call", output_to_operand_aliasing={{}: (7, {})} | custom-call | flops 1000000000 | bytes 4194304 | tf_op jit(solution)/shard_map/previous_group/pallas_call | solution.py:257
Async XLA Ops:
  0.0 5.4 %copy-start.1 = (s32[1,2,2]{2,1,0:T(2,128)S(1)}, s32[1,2,2]{2,1,0:T(2,128)}, u32[]{:S(2)}) copy-start(s32[1,2,2]{2,1,0:T(2,128)} %length_ref.1) | copy-start | bytes 52
  0.0 2.4 %copy-start.2 = (bf16[1,2,2,64,896]{4,3,2,1,0:T(8,128)(2,1)S(1)}, bf16[1,2,2,64,896]{4,3,2,1,0:T(8,128)(2,1)}, u32[]{:S(2)}) copy-start(bf16[1,2,2,64,896]{4,3,2,1,0:T(8,128)(2,1)} %enc_hbm.1) | copy-start | bytes 1376260
  0.0 5.4 %copy-start = (bf16[1,128,1024]{2,1,0:T(8,128)(2,1)S(1)}, bf16[1,128,1024]{2,1,0:T(8,128)(2,1)}, u32[]{:S(2)}) copy-start(bf16[1,128,1024]{2,1,0:T(8,128)(2,1)} %query_ref.1) | copy-start | bytes 786436
  1.0 10.1 %collective-permute-start = (bf16[2,64,896]{2,1,0:T(8,128)(2,1)S(1)}, bf16[2,64,896]{2,1,0:T(8,128)(2,1)S(1)}, u32[]{:S(2)}, u32[]{:S(2)}) collective-permute-start(bf16[2,64,896]{2,1,0:T(8,128)(2,1)S(1)} %payload.1), channel_id=1, source_target_pairs={{0,2},{2,4},{4,6},{6,8},{8,10},{10,12},{12,14},{14,16},{16,18},{18... | collective-permute-start | bytes 688136 | tf_op jit(solution)/shard_map/ppermute | solution.py:214
  11.2 2.7 %collective-permute-start.1 = (bf16[2,64,896]{2,1,0:T(8,128)(2,1)S(1)}, bf16[2,64,896]{2,1,0:T(8,128)(2,1)S(1)}, u32[]{:S(2)}, u32[]{:S(2)}) collective-permute-start(bf16[2,64,896]{2,1,0:T(8,128)(2,1)S(1)} %collective-permute-done.own_ref), channel_id=1, source_target_pairs={{0,1},{1,0},{2,3},{3,2},{4,5},{5,4},{6,7},{7,6},{8,9},{9,8},{10,11... | collective-permute-start | bytes 688136 | tf_op jit(solution)/shard_map/ppermute | solution.py:243

commit v4 on v3

--- a/solution.py
+++ b/solution.py
@@ -36,10 +36,10 @@
 
 def payload_kernel(length_hbm, enc_hbm, out_ref, length_ref, sems):
     group_count, neighbours, nb_half, _ = enc_hbm.shape[1:]
-    quarters = [(n, pl.ds(i * nb_half // 2, nb_half // 2)) for n in range(neighbours) for i in range(2)]
+    rows = [pl.ds(n * nb_half, nb_half) for n in range(neighbours)]
     copies = [
-        pltpu.make_async_copy(enc_hbm.at[0, group_count - 1].at[part], out_ref.at[part], sems.at[i])
-        for i, part in enumerate(quarters)
+        pltpu.make_async_copy(enc_hbm.at[0, group_count - 1, n], out_ref.at[rows[n]], sems.at[n])
+        for n in range(neighbours)
     ]
     lengths = pltpu.make_async_copy(length_hbm, length_ref, sems.at[len(copies)])
     lengths.start()
@@ -52,22 +52,24 @@
     for copy in copies:
         copy.wait()
     for n in range(neighbours):
-        part = out_ref[n, :, :128].astype(jnp.float32)
-        out_ref[n, :, :128] = jnp.where(marks[n], DEAD, part).astype(jnp.bfloat16)
+        part = out_ref[rows[n], :128].astype(jnp.float32)
+        out_ref[rows[n], :128] = jnp.where(marks[n], DEAD, part).astype(jnp.bfloat16)
 
 
 def local_kernel(
-    length_ref, query_ref, enc_ref, kw_hbm, vw_hbm, out_hbm, edge_ref, map_ref, vw_ref,
-    kw_ref, key_ref, value_ref, score_ref, max_ref, weight_ref, out_ref, sems,
+    length_ref, enc_ref, query_hbm, kw_hbm, vw_hbm, out_hbm, edge_ref, map_ref, vw_ref,
+    query_ref, kw_ref, key_ref, value_ref, score_ref, max_ref, weight_ref, out_ref, sems,
 ):
-    tok_count, col_count = query_ref.shape[1:]
+    tok_count, col_count = query_ref.shape
     head_count = col_count // HEAD_DIM
     neighbours, nb_half, enc_width = enc_ref.shape[3:]
     half = neighbours * nb_half
     glen = tok_count // 2
     heads = [slice(start, start + HEAD_DIM) for start in range(0, col_count, HEAD_DIM)]
 
-    parts = sems.shape[1]
+    parts = sems.shape[1] - 1
+    query_copy = pltpu.make_async_copy(query_hbm.at[0], query_ref, sems.at[0, parts])
+    query_copy.start()
     depth = enc_width // parts
     copies = [
         [
@@ -91,7 +93,8 @@
             live = live | ((key >= first) & (key < end))
         return jnp.concatenate(rows, axis=0), jnp.logical_not(live)
 
-    query = query_ref[0].astype(jnp.float32)
+    query_copy.wait()
+    query = query_ref[...].astype(jnp.float32)
     row = lax.broadcasted_iota(jnp.int32, (glen, 1), 0)
     halo_query = jnp.where(row < glen - 1, query[:glen], query[tok_count - 1 :]).astype(jnp.bfloat16)
     query = pltpu.roll(query, 1, 0)[glen:].astype(jnp.bfloat16)
@@ -145,7 +148,7 @@
 
 
 def own_kernel(glen, own_ref, map_ref, vw_ref, value_ref, score_ref, max_ref):
-    own = own_ref[...].reshape(-1, own_ref.shape[-1])
+    own = own_ref[...]
     value_ref[...] = dot(own, vw_ref[...]).astype(jnp.bfloat16)
     score_ref[...] = dot_nt(map_ref[...], own)
     dead = score_ref[glen - 1 : glen, :] > DEAD - 1.0
@@ -165,7 +168,7 @@
 
     @pl.when(lax.axis_index(AXES) > 0)
     def _():
-        other = other_ref[...].reshape(half, -1)
+        other = other_ref[...]
         score_ref[...] = dot_nt(map_ref[...], other)
         other_value = dot(other, vw_ref[...]).astype(jnp.bfloat16)
         dead = score_ref[glen - 1 : glen, :] > DEAD - 1.0
@@ -202,18 +205,18 @@
 
     payload = pl.pallas_call(
         payload_kernel,
-        out_shape=jax.ShapeDtypeStruct((neighbours, nb_half, enc_width), jnp.bfloat16),
+        out_shape=pltpu.VMEM((half, enc_width), jnp.bfloat16),
         in_specs=[hbm, hbm],
         out_specs=vmem,
-        scratch_shapes=[pltpu.SMEM(neighbour_lengths.shape, jnp.int32), pltpu.SemaphoreType.DMA((2 * neighbours + 1,))],
-        compiler_params=pltpu.CompilerParams(vmem_limit_bytes=4 * 2**20),
+        scratch_shapes=[pltpu.SMEM(neighbour_lengths.shape, jnp.int32), pltpu.SemaphoreType.DMA((neighbours + 1,))],
+        compiler_params=pltpu.CompilerParams(vmem_limit_bytes=127 * 2**19),
         cost_estimate=pl.CostEstimate(flops=10**10, bytes_accessed=2**20, transcendentals=0),
         name="payload",
     )(*(pltpu.with_memory_space_constraint(x, pltpu.HBM) for x in (neighbour_lengths, encodings)))
     size = lax.axis_size(AXES)
     halo = lax.ppermute(payload, AXES, [(i, (i + 1) % size) for i in range(size)])
     enc = lax.all_gather(encodings, "grp", axis=0)
-    key_weight, value_weight = (pltpu.with_memory_space_constraint(x, pltpu.HBM) for x in (key_weight, value_weight))
+    fetched = (pltpu.with_memory_space_constraint(x, pltpu.HBM) for x in (queries, key_weight, value_weight))
     out, edge, mapped, value_weight = pl.pallas_call(
         local_kernel,
         out_shape=[
@@ -222,9 +225,10 @@
             jax.ShapeDtypeStruct((rows, enc_width), jnp.bfloat16),
             jax.ShapeDtypeStruct(value_weight.shape, jnp.bfloat16),
         ],
-        in_specs=[vmem] * 3 + [hbm] * 2,
+        in_specs=[vmem] * 2 + [hbm] * 3,
         out_specs=[hbm] + [vmem] * 3,
         scratch_shapes=[
+            pltpu.VMEM((tok_count, col_count), jnp.bfloat16),
             pltpu.VMEM(key_weight.shape, jnp.bfloat16),
             pltpu.VMEM((2 * half, col_count), jnp.bfloat16),
             pltpu.VMEM((2 * half, col_count), jnp.bfloat16),
@@ -232,12 +236,12 @@
             pltpu.VMEM((rows, 128), jnp.float32),
             pltpu.VMEM((rows, 2 * half), jnp.bfloat16),
             pltpu.VMEM((tok_count, col_count), jnp.bfloat16),
-            pltpu.SemaphoreType.DMA((2, 4)),
+            pltpu.SemaphoreType.DMA((2, 5)),
         ],
         compiler_params=params,
         cost_estimate=pl.CostEstimate(flops=2 * 10**9, bytes_accessed=6 * 2**20, transcendentals=0),
         name="local_groups",
-    )(neighbour_lengths, queries, enc, key_weight, value_weight)
+    )(neighbour_lengths, enc, *fetched)
 
     halo, out, mapped = lax.optimization_barrier((halo, out, mapped))
     halo_other = lax.ppermute(halo, "grp", [(0, 1), (1, 0)])

time: 15.6 us -> 15.6 us (level)
  waiting for transfers between devices: 0.83 us -> 0.53 us
  blocking collectives: 3.03 us -> 3.24 us
    ppermute x1, waiting for transfers between devices: 0.49 us -> 0.2 us  [shards(): lax.ppermute(payload, AXES, [(i, (i + 1) % size) for i in range(size)])]
    all_gather x1, blocking collectives: 3.03 us -> 3.24 us  [shards(): enc = lax.all_gather(encodings, 'grp', axis=0)]
  transfers between devices with their start and end apart: 2 -> 2, of which waited for: 2 -> 2; matrix products, arithmetic and copies ran while one was open for 0% -> 0% of each run, Pallas kernels for 39% -> 40%
where the time goes in v4:
time: 15.6 us; the launch traced here: 15.4 us
  Pallas kernels  8.73 us (56%)
  blocking collectives  3.24 us (21%)
  starting transfers between devices  2.9 us (19%)
  waiting for transfers between devices  0.53 us (3%)
    pallas_call x1, Pallas kernels, shards(): pl.pallas_call(local_kernel, out_shape=[jax.ShapeDtypeStruct(queries.shap...  5.32 us
    all_gather x1, blocking collectives, shards(): enc = lax.all_gather(encodings, 'grp', axis=0)  3.24 us
    pallas_call x1, Pallas kernels, shards(): pl.pallas_call(halo_kernel, out_shape=jax.ShapeDtypeStruct(queries.shape,...  1.64 us
    ppermute x1, starting transfers between devices, shards(): halo_other = lax.ppermute(halo, 'grp', [(0, 1), (1, 0)])  1.55 us
    ppermute x1, starting transfers between devices, shards(): lax.ppermute(payload, AXES, [(i, (i + 1) % size) for i in range(size)])  1.35 us
    pallas_call x1, Pallas kernels, shards(): pl.pallas_call(payload_kernel, out_shape=pltpu.VMEM((half, enc_width), jn...  1 us
    pallas_call x1, Pallas kernels, shards(): pl.pallas_call(functools.partial(own_kernel, glen), out_shape=[jax.ShapeD...  0.78 us
    ppermute x1, waiting for transfers between devices, shards(): halo_other = lax.ppermute(halo, 'grp', [(0, 1), (1, 0)])  0.33 us
  transfers between devices with their start and end apart: 2, of which 2 were waited for; matrix products, arithmetic and copies ran while one was open for 0% of the time, Pallas kernels for 40%

profile of v4, /device:TPU:5, one launch (start us, length us, event | category | flops | bytes accessed | tf_op | source)
XLA Modules:
  0.0 15.4 jit_solution(11951291233243632299)
XLA Ops:
  0.0 0.0 copy-start
  0.0 1.0 %payload.1 = bf16[128,896]{1,0:T(8,128)(2,1)S(1)} custom-call(s32[1,2,2]{2,1,0:T(2,128)} %length_ref.1, bf16[1,2,2,64,896]{4,3,2,1,0:T(8,128)(2,1)} %enc_hbm.1), custom_call_target="tpu_custom_call" | custom-call | flops 10000000000 | bytes 1048576 | tf_op jit(solution)/shard_map/payload/pallas_call | solution.py:206
  1.0 1.3 %collective-permute-start = (bf16[128,896]{1,0:T(8,128)(2,1)S(1)}, bf16[128,896]{1,0:T(8,128)(2,1)S(1)}, u32[]{:S(2)}, u32[]{:S(2)}) collective-permute-start(bf16[128,896]{1,0:T(8,128)(2,1)S(1)} %payload.1), channel_id=1, source_target_pairs={{0,2},{2,4},{4,6},{6,8},{8,10},{10,12},{12,14},{14,16},{16,18},{18... | collective-permute-start | bytes 688136 | tf_op jit(solution)/shard_map/ppermute | solution.py:217
  2.4 3.2 %all-gather = bf16[2,2,2,64,896]{4,3,2,1,0:T(8,128)(2,1)S(1)} all-gather(bf16[1,2,2,64,896]{4,3,2,1,0:T(8,128)(2,1)} %enc_hbm.1), channel_id=2, replica_groups=mesh['seq'=4,'fsdp'=4,'grp'=2] {'grp'}, dimensions={0}, use_global_device_ids=true | all-gather | bytes 1376256 | tf_op jit(solution)/shard_map/all_gather | solution.py:218
  5.6 0.0 copy-done
  5.6 5.3 %local_groups.1 = (bf16[1,128,1024]{2,1,0:T(8,128)(2,1)}, f32[1,1024]{1,0:T(1,128)S(1)}, bf16[512,896]{1,0:T(8,128)(2,1)S(1)}, bf16[896,1024]{1,0:T(8,128)(2,1)S(1)}) custom-call(s32[1,2,2]{2,1,0:T(2,128)S(1)} %copy-done, bf16[2,1,2,2,64,896]{5,4,3,2,1,0:T(8,128)(2,1)S(1)} %bitcast.1, bf16[1,128,1024]{2,1,0:T(8,128)(2,1)} %query_hbm.1, ...), custom_call_target="tpu_custom_call" | custom-call | flops 2000000000 | bytes 6291456 | tf_op jit(solution)/shard_map/local_groups/pallas_call | solution.py:220
  10.9 0.2 %collective-permute-done.own_ref = bf16[128,896]{1,0:T(8,128)(2,1)S(1)} collective-permute-done((bf16[128,896]{1,0:T(8,128)(2,1)S(1)}, bf16[128,896]{1,0:T(8,128)(2,1)S(1)}, u32[]{:S(2)}, u32[]{:S(2)}) %collective-permute-start) | collective-permute-done | bytes 229408 | tf_op jit(solution)/shard_map/ppermute | solution.py:217
  11.1 1.5 %collective-permute-start.1 = (bf16[128,896]{1,0:T(8,128)(2,1)S(1)}, bf16[128,896]{1,0:T(8,128)(2,1)S(1)}, u32[]{:S(2)}, u32[]{:S(2)}) collective-permute-start(bf16[128,896]{1,0:T(8,128)(2,1)S(1)} %collective-permute-done.own_ref), channel_id=1, source_target_pairs={{0,1},{1,0},{2,3},{3,2},{4,5},{5,4},{6,7},{7,6},{8,9},{9,8},{10,11... | collective-permute-start | bytes 688136 | tf_op jit(solution)/shard_map/ppermute | solution.py:247
  12.7 0.8 %own_half.1 = (bf16[128,1024]{1,0:T(8,128)(2,1)S(1)}, f32[512,128]{1,0:T(8,128)S(1)}, f32[512,128]{1,0:T(8,128)S(1)}) custom-call(bf16[128,896]{1,0:T(8,128)(2,1)S(1)} %collective-permute-done.own_ref, bf16[512,896]{1,0:T(8,128)(2,1)S(1)} %get-tuple-element.18.map_ref, bf16[896,1024]{1,0:T(8,128)(2,1)S(1)} %get-tuple-element.19.vw_ref), custom_call_target="tpu_custom_call" | custom-call | flops 300000000 | bytes 1048576 | tf_op jit(solution)/shard_map/own_half/pallas_call | solution.py:248
  13.5 0.3 %collective-permute-done.1.other_ref = bf16[128,896]{1,0:T(8,128)(2,1)S(1)} collective-permute-done((bf16[128,896]{1,0:T(8,128)(2,1)S(1)}, bf16[128,896]{1,0:T(8,128)(2,1)S(1)}, u32[]{:S(2)}, u32[]{:S(2)}) %collective-permute-start.1) | collective-permute-done | bytes 229408 | tf_op jit(solution)/shard_map/ppermute | solution.py:247
  13.8 1.6 %previous_group.1 = bf16[1,128,1024]{2,1,0:T(8,128)(2,1)} custom-call(bf16[128,896]{1,0:T(8,128)(2,1)S(1)} %collective-permute-done.1.other_ref, bf16[128,1024]{1,0:T(8,128)(2,1)S(1)} %get-tuple-element.20.own_value_ref, f32[512,128]{1,0:T(8,128)S(1)} %get-tuple-element.21.own_score_ref, ...), custom_call_target="tpu_custom_call", output_to_operand_aliasing={{}: (7, {})} | custom-call | flops 1000000000 | bytes 4194304 | tf_op jit(solution)/shard_map/previous_group/pallas_call | solution.py:261
Async XLA Ops:
  0.0 5.6 %copy-start = (s32[1,2,2]{2,1,0:T(2,128)S(1)}, s32[1,2,2]{2,1,0:T(2,128)}, u32[]{:S(2)}) copy-start(s32[1,2,2]{2,1,0:T(2,128)} %length_ref.1) | copy-start | bytes 52
  1.0 10.1 %collective-permute-start = (bf16[128,896]{1,0:T(8,128)(2,1)S(1)}, bf16[128,896]{1,0:T(8,128)(2,1)S(1)}, u32[]{:S(2)}, u32[]{:S(2)}) collective-permute-start(bf16[128,896]{1,0:T(8,128)(2,1)S(1)} %payload.1), channel_id=1, source_target_pairs={{0,2},{2,4},{4,6},{6,8},{8,10},{10,12},{12,14},{14,16},{16,18},{18... | collective-permute-start | bytes 688136 | tf_op jit(solution)/shard_map/ppermute | solution.py:217
  11.1 2.7 %collective-permute-start.1 = (bf16[128,896]{1,0:T(8,128)(2,1)S(1)}, bf16[128,896]{1,0:T(8,128)(2,1)S(1)}, u32[]{:S(2)}, u32[]{:S(2)}) collective-permute-start(bf16[128,896]{1,0:T(8,128)(2,1)S(1)} %collective-permute-done.own_ref), channel_id=1, source_target_pairs={{0,1},{1,0},{2,3},{3,2},{4,5},{5,4},{6,7},{7,6},{8,9},{9,8},{10,11... | collective-permute-start | bytes 688136 | tf_op jit(solution)/shard_map/ppermute | solution.py:247

commit v5 on v4

--- a/solution.py
+++ b/solution.py
@@ -1,4 +1,3 @@
-import functools
 import math
 
 import jax
@@ -30,7 +29,10 @@
 
 def mix(weights, rows):
     ones = jnp.ones((rows.shape[0], 128), jnp.bfloat16)
-    mixed = dot(weights, jnp.concatenate([rows, ones], axis=1))
+    return dot(weights, jnp.concatenate([rows, ones], axis=1))
+
+
+def scaled(mixed):
     return mixed[:, :-128] * (1.0 / mixed[:, -1:])
 
 
@@ -57,8 +59,8 @@
 
 
 def local_kernel(
-    length_ref, enc_ref, query_hbm, kw_hbm, vw_hbm, out_hbm, edge_ref, map_ref, vw_ref,
-    query_ref, kw_ref, key_ref, value_ref, score_ref, max_ref, weight_ref, out_ref, sems,
+    length_ref, enc_ref, query_hbm, kw_hbm, vw_hbm, out_hbm, edge_ref, map_ref, query_ref, kw_ref, vw_ref,
+    key_ref, value_ref, score_ref, max_ref, weight_ref, out_ref, sems,
 ):
     tok_count, col_count = query_ref.shape
     head_count = col_count // HEAD_DIM
@@ -117,7 +119,7 @@
 
     last_enc, last_dead = group(1)
     last_weights = softmax_weights(dot_nt(last.astype(jnp.bfloat16), last_enc), last_dead)
-    last = mix(last_weights, last_enc).astype(jnp.bfloat16)
+    last = scaled(mix(last_weights, last_enc)).astype(jnp.bfloat16)
 
     blocks = [pl.ds(start, 32) for start in range(0, head_count * glen, 32)]
     for block in blocks:
@@ -137,7 +139,7 @@
     last_out = values[2 * half :]
     token = lax.broadcasted_iota(jnp.int32, (tok_count, 1), 0)
     for h, cols in enumerate(heads):
-        out = mix(weight_ref[pl.ds(h * glen, glen), :], value_ref[:, cols])
+        out = scaled(mix(weight_ref[pl.ds(h * glen, glen), :], value_ref[:, cols]))
         first = jnp.broadcast_to(last_out[h : h + 1, cols], (glen, HEAD_DIM))
         out = pltpu.roll(jnp.concatenate([first, out], axis=0), tok_count - 1, 0)
         edge_ref[:, cols] = out[glen - 1 : glen]
@@ -147,46 +149,77 @@
     copy.wait()
 
 
-def own_kernel(glen, own_ref, map_ref, vw_ref, value_ref, score_ref, max_ref):
+def early_kernel(own_ref, kw_ref, vw_ref, key_ref, value_ref):
+    @pl.when(lax.axis_index("grp") == 1)
+    def _():
+        key_ref[...] = dot(own_ref[...], kw_ref[...]).astype(jnp.bfloat16)
+        value_ref[...] = dot(own_ref[...], vw_ref[...]).astype(jnp.bfloat16)
+
+
+def own_kernel(
+    own_ref, query_ref, kw_ref, vw_ref, early_key_ref, early_value_ref, mix_ref, max_ref,
+    key_ref, value_ref, score_ref, weight_ref,
+):
     own = own_ref[...]
-    value_ref[...] = dot(own, vw_ref[...]).astype(jnp.bfloat16)
-    score_ref[...] = dot_nt(map_ref[...], own)
-    dead = score_ref[glen - 1 : glen, :] > DEAD - 1.0
-    for start in range(0, score_ref.shape[0], 32):
-        block = pl.ds(start, 32)
+    glen = query_ref.shape[0] // 2
+    heads = [slice(start, start + HEAD_DIM) for start in range(0, query_ref.shape[1], HEAD_DIM)]
+    blocks = [pl.ds(start, 32) for start in range(0, score_ref.shape[0], 32)]
+    early = lax.axis_index("grp") == 1
+
+    @pl.when(early)
+    def _():
+        key_ref[...] = early_key_ref[...]
+        value_ref[...] = early_value_ref[...]
+
+    @pl.when(jnp.logical_not(early))
+    def _():
+        key_ref[...] = dot(own, kw_ref[...]).astype(jnp.bfloat16)
+        value_ref[...] = dot(own, vw_ref[...]).astype(jnp.bfloat16)
+
+    for h, cols in enumerate(heads):
+        score_ref[pl.ds(h * glen, glen), :] = dot_nt(query_ref[:glen, cols], key_ref[:, cols]) * SCORE_SCALE
+    lane = lax.broadcasted_iota(jnp.int32, (16, 128), 1)
+    first_column = dot_nt(jnp.where(lane == 0, 1.0, 0.0).astype(jnp.bfloat16), own[:, :128])
+    dead = first_column[0:1] > DEAD - 1.0
+    for block in blocks:
         scores = jnp.where(dead, MASK_FILL, score_ref[block, :])
-        score_ref[block, :] = scores
         max_ref[block, :] = jnp.broadcast_to(jnp.max(scores, axis=-1, keepdims=True), scores.shape)
+    for block in blocks:
+        scores = jnp.where(dead, MASK_FILL, score_ref[block, :])
+        weight_ref[block, :] = jnp.exp2(scores - max_ref[block, :]).astype(jnp.bfloat16)
+    for h, cols in enumerate(heads):
+        rows = pl.ds(h * glen, glen)
+        mix_ref[rows, :] = mix(weight_ref[rows, :], value_ref[:, cols])
 
 
 def halo_kernel(
-    other_ref, own_value_ref, own_score_ref, own_max_ref, map_ref, vw_ref, edge_ref, _, out_hbm,
-    score_ref, max_ref, weight_ref, top_ref, sem,
+    other_ref, own_mix_ref, own_max_ref, map_ref, vw_ref, edge_ref, _, out_hbm,
+    value_ref, score_ref, own_scale_ref, weight_ref, top_ref, sem,
 ):
     glen, col_count = top_ref.shape
     row_count, half = score_ref.shape
+    heads = [slice(start, start + HEAD_DIM) for start in range(0, col_count, HEAD_DIM)]
+    blocks = [pl.ds(start, 32) for start in range(0, row_count, 32)]
 
     @pl.when(lax.axis_index(AXES) > 0)
     def _():
         other = other_ref[...]
         score_ref[...] = dot_nt(map_ref[...], other)
-        other_value = dot(other, vw_ref[...]).astype(jnp.bfloat16)
+        value_ref[...] = dot(other, vw_ref[...]).astype(jnp.bfloat16)
         dead = score_ref[glen - 1 : glen, :] > DEAD - 1.0
-        blocks = [pl.ds(start, 32) for start in range(0, row_count, 32)]
         for block in blocks:
             scores = jnp.where(dead, MASK_FILL, score_ref[block, :])
             own_max = own_max_ref[block, :]
-            max_ref[block, :] = jnp.maximum(own_max, jnp.max(scores, axis=-1, keepdims=True))
-        for block in blocks:
-            top = max_ref[block, :]
-            weight_ref[block, :half] = jnp.exp2(own_score_ref[block, :] - top).astype(jnp.bfloat16)
-            scores = jnp.where(dead, MASK_FILL, score_ref[block, :])
-            weight_ref[block, half:] = jnp.exp2(scores - top).astype(jnp.bfloat16)
+            top = jnp.maximum(own_max, jnp.max(scores, axis=-1, keepdims=True))
+            own_scale_ref[block, :] = jnp.exp2(own_max - top)
+            weight_ref[block, :] = jnp.exp2(scores - top).astype(jnp.bfloat16)
         row = lax.broadcasted_iota(jnp.int32, (glen, 1), 0)
-        for start in range(0, col_count, HEAD_DIM):
-            cols = slice(start, start + HEAD_DIM)
-            value = jnp.concatenate([own_value_ref[:, cols], other_value[:, cols]], axis=0)
-            out = mix(weight_ref[pl.ds(start // HEAD_DIM * glen, glen), :], value)
+        for h, cols in enumerate(heads):
+            rows = pl.ds(h * glen, glen)
+            mixed = mix(weight_ref[rows, :], value_ref[:, cols])
+            scale = own_scale_ref[rows, :]
+            total = own_mix_ref[rows, HEAD_DIM:] * scale + mixed[:, HEAD_DIM:]
+            out = (own_mix_ref[rows, :HEAD_DIM] * scale + mixed[:, :HEAD_DIM]) * (1.0 / total)
             top_ref[:, cols] = jnp.where(row < glen - 1, out, edge_ref[:, cols]).astype(jnp.bfloat16)
         copy = pltpu.make_async_copy(top_ref, out_hbm.at[0, pl.ds(0, glen)], sem)
         copy.start()
@@ -217,19 +250,19 @@
     halo = lax.ppermute(payload, AXES, [(i, (i + 1) % size) for i in range(size)])
     enc = lax.all_gather(encodings, "grp", axis=0)
     fetched = (pltpu.with_memory_space_constraint(x, pltpu.HBM) for x in (queries, key_weight, value_weight))
-    out, edge, mapped, value_weight = pl.pallas_call(
+    out, edge, mapped, queries, key_weight, value_weight = pl.pallas_call(
         local_kernel,
         out_shape=[
             jax.ShapeDtypeStruct(queries.shape, jnp.bfloat16),
             jax.ShapeDtypeStruct((1, col_count), jnp.float32),
             jax.ShapeDtypeStruct((rows, enc_width), jnp.bfloat16),
+            jax.ShapeDtypeStruct((tok_count, col_count), jnp.bfloat16),
+            jax.ShapeDtypeStruct(key_weight.shape, jnp.bfloat16),
             jax.ShapeDtypeStruct(value_weight.shape, jnp.bfloat16),
         ],
         in_specs=[vmem] * 2 + [hbm] * 3,
-        out_specs=[hbm] + [vmem] * 3,
+        out_specs=[hbm] + [vmem] * 5,
         scratch_shapes=[
-            pltpu.VMEM((tok_count, col_count), jnp.bfloat16),
-            pltpu.VMEM(key_weight.shape, jnp.bfloat16),
             pltpu.VMEM((2 * half, col_count), jnp.bfloat16),
             pltpu.VMEM((2 * half, col_count), jnp.bfloat16),
             pltpu.VMEM((rows, 2 * half), jnp.float32),
@@ -243,39 +276,55 @@
         name="local_groups",
     )(neighbour_lengths, enc, *fetched)
 
-    halo, out, mapped = lax.optimization_barrier((halo, out, mapped))
+    halo, out, queries = lax.optimization_barrier((halo, out, queries))
+    early = pl.pallas_call(
+        early_kernel,
+        out_shape=[jax.ShapeDtypeStruct((half, col_count), jnp.bfloat16)] * 2,
+        in_specs=[vmem] * 3,
+        out_specs=[vmem] * 2,
+        compiler_params=params,
+        cost_estimate=pl.CostEstimate(flops=5 * 10**8, bytes_accessed=2**20, transcendentals=0),
+        name="early_half",
+    )(halo, key_weight, value_weight)
+    halo, early = lax.optimization_barrier((halo, early))
     halo_other = lax.ppermute(halo, "grp", [(0, 1), (1, 0)])
-    own_value, own_score, own_max = pl.pallas_call(
-        functools.partial(own_kernel, glen),
+    own_mix, own_max = pl.pallas_call(
+        own_kernel,
         out_shape=[
-            jax.ShapeDtypeStruct((half, col_count), jnp.bfloat16),
+            jax.ShapeDtypeStruct((rows, HEAD_DIM + 128), jnp.float32),
             jax.ShapeDtypeStruct((rows, half), jnp.float32),
-            jax.ShapeDtypeStruct((rows, half), jnp.float32),
-        ],
-        in_specs=[vmem] * 3,
-        out_specs=[vmem] * 3,
+        ],
+        in_specs=[vmem] * 6,
+        out_specs=[vmem] * 2,
+        scratch_shapes=[
+            pltpu.VMEM((half, col_count), jnp.bfloat16),
+            pltpu.VMEM((half, col_count), jnp.bfloat16),
+            pltpu.VMEM((rows, half), jnp.float32),
+            pltpu.VMEM((rows, half), jnp.bfloat16),
+        ],
         compiler_params=params,
-        cost_estimate=pl.CostEstimate(flops=3 * 10**8, bytes_accessed=2**20, transcendentals=0),
+        cost_estimate=pl.CostEstimate(flops=5 * 10**8, bytes_accessed=2**20, transcendentals=0),
         name="own_half",
-    )(halo, mapped, value_weight)
+    )(halo, queries, key_weight, value_weight, *early)
     return pl.pallas_call(
         halo_kernel,
-        out_shape=jax.ShapeDtypeStruct(queries.shape, jnp.bfloat16),
-        in_specs=[vmem] * 7 + [hbm],
+        out_shape=jax.ShapeDtypeStruct(out.shape, jnp.bfloat16),
+        in_specs=[vmem] * 6 + [hbm],
         out_specs=hbm,
         scratch_shapes=[
+            pltpu.VMEM((half, col_count), jnp.bfloat16),
             pltpu.VMEM((rows, half), jnp.float32),
             pltpu.VMEM((rows, half), jnp.float32),
-            pltpu.VMEM((rows, 2 * half), jnp.bfloat16),
+            pltpu.VMEM((rows, half), jnp.bfloat16),
             pltpu.VMEM((glen, col_count), jnp.bfloat16),
             pltpu.SemaphoreType.DMA,
         ],
-        input_output_aliases={7: 0},
+        input_output_aliases={6: 0},
         compiler_params=params,
         cost_estimate=pl.CostEstimate(flops=10**9, bytes_accessed=4 * 2**20, transcendentals=0),
         name="previous_group",
     )(
-        halo_other, own_value, own_score, own_max, mapped, value_weight, edge,
+        halo_other, own_mix, own_max, mapped, value_weight, edge,
         pltpu.with_memory_space_constraint(out, pltpu.HBM),
     )
 

time: 15.6 us -> 15.5 us (level)
  starting transfers between devices: 2.9 us -> 2.16 us
  Pallas kernels: 8.73 us -> 9.32 us
    ppermute x1, starting transfers between devices: 1.55 us -> 0.81 us  [shards(): halo_other = lax.ppermute(halo, 'grp', [(0, 1), (1, 0)])]
    pallas_call x2 -> x3, Pallas kernels: 2.41 us -> 2.99 us  [the longest x1 1.59 us: shards(): pl.pallas_call(halo_kernel, out_shape=jax.ShapeDtypeStruct(out.shape, jnp...]
  transfers between devices with their start and end apart: 2 -> 2, of which waited for: 2 -> 2; matrix products, arithmetic and copies ran while one was open for 0% -> 0% of each run, Pallas kernels for 40% -> 39%
where the time goes in v5:
time: 15.5 us; the launch traced here: 15.4 us
  Pallas kernels  9.32 us (60%)
  blocking collectives  3.24 us (21%)
  starting transfers between devices  2.16 us (14%)
  waiting for transfers between devices  0.63 us (4%)
    pallas_call x1, Pallas kernels, shards(): pl.pallas_call(local_kernel, out_shape=[jax.ShapeDtypeStruct(queries.shap...  5.32 us
    all_gather x1, blocking collectives, shards(): enc = lax.all_gather(encodings, 'grp', axis=0)  3.24 us
    pallas_call x1, Pallas kernels, shards(): pl.pallas_call(halo_kernel, out_shape=jax.ShapeDtypeStruct(out.shape, jnp...  1.59 us
    ppermute x1, starting transfers between devices, shards(): lax.ppermute(payload, AXES, [(i, (i + 1) % size) for i in range(size)])  1.35 us
    pallas_call x1, Pallas kernels, shards(): pl.pallas_call(payload_kernel, out_shape=pltpu.VMEM((half, enc_width), jn...  1 us
    ppermute x1, starting transfers between devices, shards(): halo_other = lax.ppermute(halo, 'grp', [(0, 1), (1, 0)])  0.81 us
    pallas_call x1, Pallas kernels, shards(): pl.pallas_call(early_kernel, out_shape=[jax.ShapeDtypeStruct((half, col_c...  0.73 us
    pallas_call x1, Pallas kernels, shards(): pl.pallas_call(own_kernel, out_shape=[jax.ShapeDtypeStruct((rows, HEAD_DI...  0.68 us
  transfers between devices with their start and end apart: 2, of which 2 were waited for; matrix products, arithmetic and copies ran while one was open for 0% of the time, Pallas kernels for 39%

profile of v5, /device:TPU:5, one launch (start us, length us, event | category | flops | bytes accessed | tf_op | source)
XLA Modules:
  0.0 15.4 jit_solution(13859797725966837601)
XLA Ops:
  0.0 0.0 copy-start
  0.0 1.0 %payload.1 = bf16[128,896]{1,0:T(8,128)(2,1)S(1)} custom-call(s32[1,2,2]{2,1,0:T(2,128)} %length_ref.1, bf16[1,2,2,64,896]{4,3,2,1,0:T(8,128)(2,1)} %enc_hbm.1), custom_call_target="tpu_custom_call" | custom-call | flops 10000000000 | bytes 1048576 | tf_op jit(solution)/shard_map/payload/pallas_call | solution.py:239
  1.0 1.3 %collective-permute-start = (bf16[128,896]{1,0:T(8,128)(2,1)S(1)}, bf16[128,896]{1,0:T(8,128)(2,1)S(1)}, u32[]{:S(2)}, u32[]{:S(2)}) collective-permute-start(bf16[128,896]{1,0:T(8,128)(2,1)S(1)} %payload.1), channel_id=1, source_target_pairs={{0,2},{2,4},{4,6},{6,8},{8,10},{10,12},{12,14},{14,16},{16,18},{18... | collective-permute-start | bytes 688136 | tf_op jit(solution)/shard_map/ppermute | solution.py:250
  2.4 3.2 %all-gather = bf16[2,2,2,64,896]{4,3,2,1,0:T(8,128)(2,1)S(1)} all-gather(bf16[1,2,2,64,896]{4,3,2,1,0:T(8,128)(2,1)} %enc_hbm.1), channel_id=2, replica_groups=mesh['seq'=4,'fsdp'=4,'grp'=2] {'grp'}, dimensions={0}, use_global_device_ids=true | all-gather | bytes 1376256 | tf_op jit(solution)/shard_map/all_gather | solution.py:251
  5.6 0.0 copy-done
  5.6 5.3 %local_groups.1 = (bf16[1,128,1024]{2,1,0:T(8,128)(2,1)}, f32[1,1024]{1,0:T(1,128)S(1)}, bf16[512,896]{1,0:T(8,128)(2,1)S(1)}, bf16[128,1024]{1,0:T(8,128)(2,1)S...) custom-call(s32[1,2,2]{2,1,0:T(2,128)S(1)} %copy-done, bf16[2,1,2,2,64,896]{5,4,3,2,1,0:T(8,128)(2,1)S(1)} %bitcast.1, ...), custom_call_target="tpu_custom_call" | custom-call | flops 2000000000 | bytes 6291456 | tf_op jit(solution)/shard_map/local_groups/pallas_call | solution.py:253
  10.9 0.2 %collective-permute-done.own_ref = bf16[128,896]{1,0:T(8,128)(2,1)S(1)} collective-permute-done((bf16[128,896]{1,0:T(8,128)(2,1)S(1)}, bf16[128,896]{1,0:T(8,128)(2,1)S(1)}, u32[]{:S(2)}, u32[]{:S(2)}) %collective-permute-start) | collective-permute-done | bytes 229408 | tf_op jit(solution)/shard_map/ppermute | solution.py:250
  11.1 0.7 %early_half.1 = (bf16[128,1024]{1,0:T(8,128)(2,1)S(1)}, bf16[128,1024]{1,0:T(8,128)(2,1)S(1)}) custom-call(bf16[128,896]{1,0:T(8,128)(2,1)S(1)} %collective-permute-done.own_ref, bf16[896,1024]{1,0:T(8,128)(2,1)S(1)} %get-tuple-element.24.kw_ref, bf16[896,1024]{1,0:T(8,128)(2,1)S(1)} %get-tuple-element.25.vw_ref), custom_call_target="tpu_custom_call" | custom-call | flops 500000000 | bytes 1048576 | tf_op jit(solution)/shard_map/early_half/pallas_call | solution.py:280
  11.9 0.8 %collective-permute-start.1 = (bf16[128,896]{1,0:T(8,128)(2,1)S(1)}, bf16[128,896]{1,0:T(8,128)(2,1)S(1)}, u32[]{:S(2)}, u32[]{:S(2)}) collective-permute-start(bf16[128,896]{1,0:T(8,128)(2,1)S(1)} %collective-permute-done.own_ref), channel_id=1, source_target_pairs={{0,1},{1,0},{2,3},{3,2},{4,5},{5,4},{6,7},{7,6},{8,9},{9,8},{10,11... | collective-permute-start | bytes 688136 | tf_op jit(solution)/shard_map/ppermute | solution.py:290
  12.7 0.7 %own_half.1 = (f32[512,256]{1,0:T(8,128)S(1)}, f32[512,128]{1,0:T(8,128)S(1)}) custom-call(bf16[128,896]{1,0:T(8,128)(2,1)S(1)} %collective-permute-done.own_ref, bf16[128,1024]{1,0:T(8,128)(2,1)S(1)} %get-tuple-element.29.query_ref, bf16[896,1024]{1,0:T(8,128)(2,1)S(1)} %get-tuple-element.24.kw_ref, bf16[896,1024]{1,0:T(8,128)(2,1)S(1)} %get-tuple-element.25.vw_ref, ...), custom_call_target="tpu_custom_call" | custom-call | flops 500000000 | bytes 1048576 | tf_op jit(solution)/shard_map/own_half/pallas_call | solution.py:291
  13.4 0.4 %collective-permute-done.1.other_ref = bf16[128,896]{1,0:T(8,128)(2,1)S(1)} collective-permute-done((bf16[128,896]{1,0:T(8,128)(2,1)S(1)}, bf16[128,896]{1,0:T(8,128)(2,1)S(1)}, u32[]{:S(2)}, u32[]{:S(2)}) %collective-permute-start.1) | collective-permute-done | bytes 229408 | tf_op jit(solution)/shard_map/ppermute | solution.py:290
  13.8 1.6 %previous_group.1 = bf16[1,128,1024]{2,1,0:T(8,128)(2,1)} custom-call(bf16[128,896]{1,0:T(8,128)(2,1)S(1)} %collective-permute-done.1.other_ref, f32[512,256]{1,0:T(8,128)S(1)} %get-tuple-element.32.own_mix_ref, f32[512,128]{1,0:T(8,128)S(1)} %get-tuple-element.33.own_max_ref, ...), custom_call_target="tpu_custom_call", output_to_operand_aliasing={{}: (6, {})} | custom-call | flops 1000000000 | bytes 4194304 | tf_op jit(solution)/shard_map/previous_group/pallas_call | solution.py:309
Async XLA Ops:
  0.0 5.6 %copy-start = (s32[1,2,2]{2,1,0:T(2,128)S(1)}, s32[1,2,2]{2,1,0:T(2,128)}, u32[]{:S(2)}) copy-start(s32[1,2,2]{2,1,0:T(2,128)} %length_ref.1) | copy-start | bytes 52
  1.0 10.1 %collective-permute-start = (bf16[128,896]{1,0:T(8,128)(2,1)S(1)}, bf16[128,896]{1,0:T(8,128)(2,1)S(1)}, u32[]{:S(2)}, u32[]{:S(2)}) collective-permute-start(bf16[128,896]{1,0:T(8,128)(2,1)S(1)} %payload.1), channel_id=1, source_target_pairs={{0,2},{2,4},{4,6},{6,8},{8,10},{10,12},{12,14},{14,16},{16,18},{18... | collective-permute-start | bytes 688136 | tf_op jit(solution)/shard_map/ppermute | solution.py:250
  11.9 1.9 %collective-permute-start.1 = (bf16[128,896]{1,0:T(8,128)(2,1)S(1)}, bf16[128,896]{1,0:T(8,128)(2,1)S(1)}, u32[]{:S(2)}, u32[]{:S(2)}) collective-permute-start(bf16[128,896]{1,0:T(8,128)(2,1)S(1)} %collective-permute-done.own_ref), channel_id=1, source_target_pairs={{0,1},{1,0},{2,3},{3,2},{4,5},{5,4},{6,7},{7,6},{8,9},{9,8},{10,11... | collective-permute-start | bytes 688136 | tf_op jit(solution)/shard_map/ppermute | solution.py:290

commit v6 on v5

--- a/solution.py
+++ b/solution.py
@@ -39,13 +39,18 @@
 def payload_kernel(length_hbm, enc_hbm, out_ref, length_ref, sems):
     group_count, neighbours, nb_half, _ = enc_hbm.shape[1:]
     rows = [pl.ds(n * nb_half, nb_half) for n in range(neighbours)]
+    part = nb_half // 2
     copies = [
-        pltpu.make_async_copy(enc_hbm.at[0, group_count - 1, n], out_ref.at[rows[n]], sems.at[n])
+        pltpu.make_async_copy(
+            enc_hbm.at[0, group_count - 1, n, pl.ds(i * part, part)],
+            out_ref.at[pl.ds(n * nb_half + i * part, part)],
+            sems.at[2 * n + i],
+        )
         for n in range(neighbours)
+        for i in range(2)
     ]
     lengths = pltpu.make_async_copy(length_hbm, length_ref, sems.at[len(copies)])
-    lengths.start()
-    for copy in copies:
+    for copy in copies + [lengths]:
         copy.start()
     row = lax.broadcasted_iota(jnp.int32, (nb_half, 128), 0) + lax.axis_index("grp") * nb_half
     lane = lax.broadcasted_iota(jnp.int32, (nb_half, 128), 1)
@@ -54,8 +59,8 @@
     for copy in copies:
         copy.wait()
     for n in range(neighbours):
-        part = out_ref[rows[n], :128].astype(jnp.float32)
-        out_ref[rows[n], :128] = jnp.where(marks[n], DEAD, part).astype(jnp.bfloat16)
+        marked = jnp.where(marks[n], DEAD, out_ref[rows[n], :128].astype(jnp.float32))
+        out_ref[rows[n], :128] = marked.astype(jnp.bfloat16)
 
 
 def local_kernel(
@@ -194,7 +199,7 @@
 
 def halo_kernel(
     other_ref, own_mix_ref, own_max_ref, map_ref, vw_ref, edge_ref, _, out_hbm,
-    value_ref, score_ref, own_scale_ref, weight_ref, top_ref, sem,
+    value_ref, score_ref, max_ref, own_scale_ref, weight_ref, mix_ref, top_ref, sem,
 ):
     glen, col_count = top_ref.shape
     row_count, half = score_ref.shape
@@ -211,15 +216,21 @@
             scores = jnp.where(dead, MASK_FILL, score_ref[block, :])
             own_max = own_max_ref[block, :]
             top = jnp.maximum(own_max, jnp.max(scores, axis=-1, keepdims=True))
-            own_scale_ref[block, :] = jnp.exp2(own_max - top)
+            max_ref[block, :] = top
+        for block in blocks:
+            top = max_ref[block, :]
+            own_scale_ref[block, :] = jnp.exp2(own_max_ref[block, :] - top)
+            scores = jnp.where(dead, MASK_FILL, score_ref[block, :])
             weight_ref[block, :] = jnp.exp2(scores - top).astype(jnp.bfloat16)
+        for h, cols in enumerate(heads):
+            rows = pl.ds(h * glen, glen)
+            mix_ref[rows, :] = mix(weight_ref[rows, :], value_ref[:, cols])
         row = lax.broadcasted_iota(jnp.int32, (glen, 1), 0)
         for h, cols in enumerate(heads):
             rows = pl.ds(h * glen, glen)
-            mixed = mix(weight_ref[rows, :], value_ref[:, cols])
             scale = own_scale_ref[rows, :]
-            total = own_mix_ref[rows, HEAD_DIM:] * scale + mixed[:, HEAD_DIM:]
-            out = (own_mix_ref[rows, :HEAD_DIM] * scale + mixed[:, :HEAD_DIM]) * (1.0 / total)
+            total = own_mix_ref[rows, HEAD_DIM:] * scale + mix_ref[rows, HEAD_DIM:]
+            out = (own_mix_ref[rows, :HEAD_DIM] * scale + mix_ref[rows, :HEAD_DIM]) * (1.0 / total)
             top_ref[:, cols] = jnp.where(row < glen - 1, out, edge_ref[:, cols]).astype(jnp.bfloat16)
         copy = pltpu.make_async_copy(top_ref, out_hbm.at[0, pl.ds(0, glen)], sem)
         copy.start()
@@ -241,7 +252,7 @@
         out_shape=pltpu.VMEM((half, enc_width), jnp.bfloat16),
         in_specs=[hbm, hbm],
         out_specs=vmem,
-        scratch_shapes=[pltpu.SMEM(neighbour_lengths.shape, jnp.int32), pltpu.SemaphoreType.DMA((neighbours + 1,))],
+        scratch_shapes=[pltpu.SMEM(neighbour_lengths.shape, jnp.int32), pltpu.SemaphoreType.DMA((2 * neighbours + 1,))],
         compiler_params=pltpu.CompilerParams(vmem_limit_bytes=127 * 2**19),
         cost_estimate=pl.CostEstimate(flops=10**10, bytes_accessed=2**20, transcendentals=0),
         name="payload",
@@ -315,7 +326,9 @@
             pltpu.VMEM((half, col_count), jnp.bfloat16),
             pltpu.VMEM((rows, half), jnp.float32),
             pltpu.VMEM((rows, half), jnp.float32),
+            pltpu.VMEM((rows, half), jnp.float32),
             pltpu.VMEM((rows, half), jnp.bfloat16),
+            pltpu.VMEM((rows, HEAD_DIM + 128), jnp.float32),
             pltpu.VMEM((glen, col_count), jnp.bfloat16),
             pltpu.SemaphoreType.DMA,
         ],

time: 15.5 us -> 15.5 us (level)
  no operation moved by 1% of the time
where the time goes in v6:
time: 15.5 us; the launch traced here: 15.3 us
  Pallas kernels  9.28 us (60%)
  blocking collectives  3.24 us (21%)
  starting transfers between devices  2.16 us (14%)
  waiting for transfers between devices  0.63 us (4%)
    pallas_call x1, Pallas kernels, shards(): pl.pallas_call(local_kernel, out_shape=[jax.ShapeDtypeStruct(queries.shap...  5.32 us
    all_gather x1, blocking collectives, shards(): enc = lax.all_gather(encodings, 'grp', axis=0)  3.24 us
    pallas_call x1, Pallas kernels, shards(): pl.pallas_call(halo_kernel, out_shape=jax.ShapeDtypeStruct(out.shape, jnp...  1.58 us
    ppermute x1, starting transfers between devices, shards(): lax.ppermute(payload, AXES, [(i, (i + 1) % size) for i in range(size)])  1.35 us
    pallas_call x1, Pallas kernels, shards(): pl.pallas_call(payload_kernel, out_shape=pltpu.VMEM((half, enc_width), jn...  0.97 us
    ppermute x1, starting transfers between devices, shards(): halo_other = lax.ppermute(halo, 'grp', [(0, 1), (1, 0)])  0.81 us
    pallas_call x1, Pallas kernels, shards(): pl.pallas_call(early_kernel, out_shape=[jax.ShapeDtypeStruct((half, col_c...  0.73 us
    pallas_call x1, Pallas kernels, shards(): pl.pallas_call(own_kernel, out_shape=[jax.ShapeDtypeStruct((rows, HEAD_DI...  0.68 us
  transfers between devices with their start and end apart: 2, of which 2 were waited for; matrix products, arithmetic and copies ran while one was open for 0% of the time, Pallas kernels for 39%

profile of v6, /device:TPU:5, one launch (start us, length us, event | category | flops | bytes accessed | tf_op | source)
XLA Modules:
  0.0 15.3 jit_solution(2002521148948916909)
XLA Ops:
  0.0 0.0 copy-start
  0.0 1.0 %payload.1 = bf16[128,896]{1,0:T(8,128)(2,1)S(1)} custom-call(s32[1,2,2]{2,1,0:T(2,128)} %length_ref.1, bf16[1,2,2,64,896]{4,3,2,1,0:T(8,128)(2,1)} %enc_hbm.1), custom_call_target="tpu_custom_call" | custom-call | flops 10000000000 | bytes 1048576 | tf_op jit(solution)/shard_map/payload/pallas_call | solution.py:250
  1.0 1.3 %collective-permute-start = (bf16[128,896]{1,0:T(8,128)(2,1)S(1)}, bf16[128,896]{1,0:T(8,128)(2,1)S(1)}, u32[]{:S(2)}, u32[]{:S(2)}) collective-permute-start(bf16[128,896]{1,0:T(8,128)(2,1)S(1)} %payload.1), channel_id=1, source_target_pairs={{0,2},{2,4},{4,6},{6,8},{8,10},{10,12},{12,14},{14,16},{16,18},{18... | collective-permute-start | bytes 688136 | tf_op jit(solution)/shard_map/ppermute | solution.py:261
  2.3 3.2 %all-gather = bf16[2,2,2,64,896]{4,3,2,1,0:T(8,128)(2,1)S(1)} all-gather(bf16[1,2,2,64,896]{4,3,2,1,0:T(8,128)(2,1)} %enc_hbm.1), channel_id=2, replica_groups=mesh['seq'=4,'fsdp'=4,'grp'=2] {'grp'}, dimensions={0}, use_global_device_ids=true | all-gather | bytes 1376256 | tf_op jit(solution)/shard_map/all_gather | solution.py:262
  5.6 0.0 copy-done
  5.6 5.3 %local_groups.1 = (bf16[1,128,1024]{2,1,0:T(8,128)(2,1)}, f32[1,1024]{1,0:T(1,128)S(1)}, bf16[512,896]{1,0:T(8,128)(2,1)S(1)}, bf16[128,1024]{1,0:T(8,128)(2,1)S...) custom-call(s32[1,2,2]{2,1,0:T(2,128)S(1)} %copy-done, bf16[2,1,2,2,64,896]{5,4,3,2,1,0:T(8,128)(2,1)S(1)} %bitcast.1, ...), custom_call_target="tpu_custom_call" | custom-call | flops 2000000000 | bytes 6291456 | tf_op jit(solution)/shard_map/local_groups/pallas_call | solution.py:264
  10.9 0.2 %collective-permute-done.own_ref = bf16[128,896]{1,0:T(8,128)(2,1)S(1)} collective-permute-done((bf16[128,896]{1,0:T(8,128)(2,1)S(1)}, bf16[128,896]{1,0:T(8,128)(2,1)S(1)}, u32[]{:S(2)}, u32[]{:S(2)}) %collective-permute-start) | collective-permute-done | bytes 229408 | tf_op jit(solution)/shard_map/ppermute | solution.py:261
  11.1 0.7 %early_half.1 = (bf16[128,1024]{1,0:T(8,128)(2,1)S(1)}, bf16[128,1024]{1,0:T(8,128)(2,1)S(1)}) custom-call(bf16[128,896]{1,0:T(8,128)(2,1)S(1)} %collective-permute-done.own_ref, bf16[896,1024]{1,0:T(8,128)(2,1)S(1)} %get-tuple-element.24.kw_ref, bf16[896,1024]{1,0:T(8,128)(2,1)S(1)} %get-tuple-element.25.vw_ref), custom_call_target="tpu_custom_call" | custom-call | flops 500000000 | bytes 1048576 | tf_op jit(solution)/shard_map/early_half/pallas_call | solution.py:291
  11.8 0.8 %collective-permute-start.1 = (bf16[128,896]{1,0:T(8,128)(2,1)S(1)}, bf16[128,896]{1,0:T(8,128)(2,1)S(1)}, u32[]{:S(2)}, u32[]{:S(2)}) collective-permute-start(bf16[128,896]{1,0:T(8,128)(2,1)S(1)} %collective-permute-done.own_ref), channel_id=1, source_target_pairs={{0,1},{1,0},{2,3},{3,2},{4,5},{5,4},{6,7},{7,6},{8,9},{9,8},{10,11... | collective-permute-start | bytes 688136 | tf_op jit(solution)/shard_map/ppermute | solution.py:301
  12.6 0.7 %own_half.1 = (f32[512,256]{1,0:T(8,128)S(1)}, f32[512,128]{1,0:T(8,128)S(1)}) custom-call(bf16[128,896]{1,0:T(8,128)(2,1)S(1)} %collective-permute-done.own_ref, bf16[128,1024]{1,0:T(8,128)(2,1)S(1)} %get-tuple-element.29.query_ref, bf16[896,1024]{1,0:T(8,128)(2,1)S(1)} %get-tuple-element.24.kw_ref, bf16[896,1024]{1,0:T(8,128)(2,1)S(1)} %get-tuple-element.25.vw_ref, ...), custom_call_target="tpu_custom_call" | custom-call | flops 500000000 | bytes 1048576 | tf_op jit(solution)/shard_map/own_half/pallas_call | solution.py:302
  13.3 0.4 %collective-permute-done.1.other_ref = bf16[128,896]{1,0:T(8,128)(2,1)S(1)} collective-permute-done((bf16[128,896]{1,0:T(8,128)(2,1)S(1)}, bf16[128,896]{1,0:T(8,128)(2,1)S(1)}, u32[]{:S(2)}, u32[]{:S(2)}) %collective-permute-start.1) | collective-permute-done | bytes 229408 | tf_op jit(solution)/shard_map/ppermute | solution.py:301
  13.8 1.6 %previous_group.1 = bf16[1,128,1024]{2,1,0:T(8,128)(2,1)} custom-call(bf16[128,896]{1,0:T(8,128)(2,1)S(1)} %collective-permute-done.1.other_ref, f32[512,256]{1,0:T(8,128)S(1)} %get-tuple-element.32.own_mix_ref, f32[512,128]{1,0:T(8,128)S(1)} %get-tuple-element.33.own_max_ref, ...), custom_call_target="tpu_custom_call", output_to_operand_aliasing={{}: (6, {})} | custom-call | flops 1000000000 | bytes 4194304 | tf_op jit(solution)/shard_map/previous_group/pallas_call | solution.py:320
Async XLA Ops:
  0.0 5.6 %copy-start = (s32[1,2,2]{2,1,0:T(2,128)S(1)}, s32[1,2,2]{2,1,0:T(2,128)}, u32[]{:S(2)}) copy-start(s32[1,2,2]{2,1,0:T(2,128)} %length_ref.1) | copy-start | bytes 52
  1.0 10.1 %collective-permute-start = (bf16[128,896]{1,0:T(8,128)(2,1)S(1)}, bf16[128,896]{1,0:T(8,128)(2,1)S(1)}, u32[]{:S(2)}, u32[]{:S(2)}) collective-permute-start(bf16[128,896]{1,0:T(8,128)(2,1)S(1)} %payload.1), channel_id=1, source_target_pairs={{0,2},{2,4},{4,6},{6,8},{8,10},{10,12},{12,14},{14,16},{16,18},{18... | collective-permute-start | bytes 688136 | tf_op jit(solution)/shard_map/ppermute | solution.py:261
  11.8 1.9 %collective-permute-start.1 = (bf16[128,896]{1,0:T(8,128)(2,1)S(1)}, bf16[128,896]{1,0:T(8,128)(2,1)S(1)}, u32[]{:S(2)}, u32[]{:S(2)}) collective-permute-start(bf16[128,896]{1,0:T(8,128)(2,1)S(1)} %collective-permute-done.own_ref), channel_id=1, source_target_pairs={{0,1},{1,0},{2,3},{3,2},{4,5},{5,4},{6,7},{7,6},{8,9},{9,8},{10,11... | collective-permute-start | bytes 688136 | tf_op jit(solution)/shard_map/ppermute | solution.py:301
